TPU v7x, 256 devices: a whole 4x4x8 slice. The times are simulated.
256 devices in a mesh: replica: 16 (over z, core), mp: 16 (over y, x).
Axes of the slice: x: 4, y: 4, z: 8, core: 2. Of those that a mesh axis runs over, the one named last changes fastest.
Arguments:
- pre_act: bfloat16 [2400, 32768], P('mp', 'replica'), may hold values from -6 to 6
- out_grad: bfloat16 [32768, 4800], P(('replica', 'mp')), may hold values from -6 to 6
- weight: bfloat16 [2400, 4800], P('mp'), may hold values from -0.09375 to 0.09375
- error: float32 [16, 2400, 4800], P('replica', 'mp'), may hold values from -96 to 96
- q_init: float32 [4800, 32], replicated, may hold values from -6 to 6
Outputs:
- pre_grad: bfloat16 [2400, 32768], P('mp', 'replica')
- new_error: float32 [16, 2400, 4800], P('replica', 'mp')
- q_new: float32 [4800, 32], replicated
All inputs are finite; a program needn't handle non-finite values.
Results may differ from a plain program's by a relative error of at most 0.013.
Values may be sent and summed in bfloat16 or wider, within the bound.
No kernel may reach another device: no remote copies, remote signals or barrier semaphores. Data moves between devices by JAX's collectives and lax.ppermute only.
A program may use at most 128 MiB of HBM per device.

v0:
```python
import functools

import jax
import jax.numpy as jnp
from jax import lax
from jax.experimental import pallas as pl
from jax.experimental.pallas import tpu as pltpu
from jax.sharding import Mesh, PartitionSpec as P

F32 = jnp.float32
BF16 = jnp.bfloat16
MP = ("y", "x")
ALL = ("z", "core", "y", "x")


def gelu_back(pre, grad):
    _, pull = jax.vjp(jax.nn.gelu, pre)
    return pull(grad)[0]


def gelu16(pre):
    return jax.nn.gelu(pre.astype(F32)).astype(BF16)


def split(x, parts):
    out = []
    for _ in range(parts):
        top = lax.reduce_precision(x, 8, 7)
        out.append(top.astype(BF16))
        x = x - top
    return out


def dot(a, b, ca, cb):
    return lax.dot_general(a, b, (((ca,), (cb,)), ((), ())), preferred_element_type=F32)


def fold(x, parts, axis=0):
    n = x.shape[axis] // parts
    return sum(lax.slice_in_dim(x, i * n, (i + 1) * n, axis=axis) for i in range(parts))


def spread(x, axis):
    n = lax.axis_size(axis)
    return lax.all_to_all(jnp.broadcast_to(x, (n,) + x.shape), axis, 0, 0, tiled=True)


def other_core(x):
    return lax.ppermute(x, "core", [(0, 1), (1, 0)])


def shift(x, axis, step):
    n = lax.axis_size(axis)
    return lax.ppermute(x, axis, [((i + step) % n, i) for i in range(n)])


def products(n, where, pre_ref, weight_ref, *refs):
    blocks, held, (mat_ref, grad_ref, pre_buf, weight_buf, sems) = refs[:n], refs[n:-5], refs[-5:]
    fetch_pre = pltpu.make_async_copy(pre_ref, pre_buf, sems.at[0])
    fetch_weight = pltpu.make_async_copy(weight_ref, weight_buf, sems.at[1])
    fetch_pre.start()
    fetch_weight.start()
    if held:
        grad_ref[...] = held[1][...]
    own = blocks[0].shape[1]
    spots = [pl.ds(pl.multiple_of(where[i] * own, own), own) for i in range(n)]
    fetch_pre.wait()
    pre = jnp.concatenate([pre_buf[:, s] for s in spots], axis=1).astype(F32)
    act, pull = jax.vjp(jax.nn.gelu, pre)
    act = act.astype(BF16)
    fetch_weight.wait()
    feat = weight_buf.shape[1]
    back = jnp.zeros(pre.shape, F32)
    for lo in range(0, feat, 512):
        part = slice(lo, min(feat, lo + 512))
        piece = jnp.concatenate([b[part, :] for b in blocks], axis=1)
        back = back + dot(weight_buf[:, part], piece, 1, 0)
        more = dot(act, piece, 1, 1)
        mat_ref[:, part] = more + held[0][:, part] if held else more
    out = pull(back)[0].astype(BF16)
    for i, s in enumerate(spots):
        grad_ref[:, s] = out[:, i * own:(i + 1) * own]


def add_products(where, pre_act, weight, blocks, held):
    vmem = pl.BlockSpec(memory_space=pltpu.VMEM)
    n = len(blocks)
    mat = jax.ShapeDtypeStruct(weight.shape, F32)
    return pl.pallas_call(
        functools.partial(products, n),
        out_shape=(mat, jax.ShapeDtypeStruct(pre_act.shape, BF16)),
        in_specs=[pl.BlockSpec(memory_space=pltpu.SMEM)]
        + [pl.BlockSpec(memory_space=pltpu.HBM)] * 2
        + [vmem] * (n + len(held)),
        out_specs=(vmem, vmem),
        scratch_shapes=[
            pltpu.VMEM(pre_act.shape, BF16),
            pltpu.VMEM(weight.shape, BF16),
            pltpu.SemaphoreType.DMA((2,)),
        ],
        input_output_aliases={n + 3: 0, n + 4: 1} if held else {},
        compiler_params=pltpu.CompilerParams(vmem_limit_bytes=12 * 2**20),
    )(where, pre_act, weight, *blocks, *held)


def finish(mat_ref, error_ref, left_ref, right_ref, out_ref):
    feat = mat_ref.shape[1]
    left = left_ref[...]
    for lo in range(0, feat, 512):
        part = slice(lo, min(feat, lo + 512))
        out_ref[:, 0, part] = mat_ref[:, part] + error_ref[:, 0, part] - dot(left, right_ref[:, part], 1, 0)


def new_errors(mat, error, left, right):
    vmem = pl.BlockSpec(memory_space=pltpu.VMEM)
    return pl.pallas_call(
        finish,
        out_shape=jax.ShapeDtypeStruct(error.shape, F32),
        in_specs=[vmem] * 4,
        out_specs=vmem,
        compiler_params=pltpu.CompilerParams(vmem_limit_bytes=12 * 2**20),
    )(mat, error, left, right)


def right_rows(z_ref, og_ref, more_ref, out_ref):
    rank, feat = out_ref.shape
    z = z_ref[...]
    for lo in range(0, feat, 512):
        part = slice(lo, min(feat, lo + 512))
        out_ref[:, part] = fold(dot(z, og_ref[part, :], 1, 1), 2) + more_ref[:, part]


def right_factor(z2, og, more):
    vmem = pl.BlockSpec(memory_space=pltpu.VMEM)
    return pl.pallas_call(
        right_rows,
        out_shape=jax.ShapeDtypeStruct(more.shape, F32),
        in_specs=[vmem] * 3,
        out_specs=vmem,
        compiler_params=pltpu.CompilerParams(vmem_limit_bytes=12 * 2**20),
    )(z2, og, more)


def shards(sizes, pre_act, out_grad, weight, error, q_init):
    hi = lax.Precision.HIGHEST
    nz, nc, ny, nx = sizes
    groups = nz * nc
    mp = ny * nx
    rank = q_init.shape[1]
    half = rank // 2
    hid, toks = pre_act.shape
    own, feat = out_grad.shape
    error = error[0]
    core = lax.axis_index("core")

    og = out_grad.T
    got = {(0, 0): og}
    iy, ix = lax.axis_index("y"), lax.axis_index("x")
    state = []

    def fetch(*moves):
        new = {}
        for key, axis, step in moves:
            dy, dx = (key[0] + step, key[1]) if axis == "y" else (key[0], key[1] + step)
            new[dy % ny, dx % nx] = shift(got[key[0] % ny, key[1] % nx], axis, step)
        got.update(new)
        return list(new)

    def tie(value, keys=(), with_state=False):
        out = lax.optimization_barrier([value, [got[k] for k in keys], state if with_state else []])
        got.update(zip(keys, out[1]))
        if with_state:
            state[:] = out[2]
        return out[0]

    def use(keys):
        where = jnp.stack([((iy + dy) & (ny - 1)) * nx + ((ix + dx) & (nx - 1)) for dy, dx in keys])
        state[:] = add_products(where, pre_act, weight, [got[k] for k in keys], state)

    one = fetch(((0, 0), "x", 1), ((0, 0), "x", -1), ((0, 0), "y", 1), ((0, 0), "y", -1))

    act = gelu16(pre_act)
    q2 = jnp.concatenate(split(q_init, 2), axis=1)
    y = fold(dot(q2, out_grad, 0, 1), 2)
    y_all = tie(spread(y, MP), one)
    two = fetch(((0, 1), "y", 1), ((0, -1), "y", -1), ((1, 0), "x", -1), ((-1, 0), "x", 1))
    use([(0, 0)] + one)
    y_all = y_all.transpose(1, 0, 2).reshape(rank, toks)
    y2 = jnp.concatenate(split(y_all, 2), axis=0)
    e2 = split(error, 2)
    p_err = sum(fold(dot(q2, e, 0, 1), 2) for e in e2)
    p_local = fold(dot(y2, act, 1, 1), 2) + p_err
    pbar = jnp.sum(tie(spread(p_local, "z"), [], True), axis=0)
    pbar = tie((pbar + other_core(pbar)) / groups, two)

    l2 = jnp.concatenate(split(pbar, 2), axis=0)
    r_error = fold(dot(l2, e2[0], 1, 0), 2)
    z_part = fold(dot(l2, act, 1, 0), 2)
    gram_part = jnp.dot(pbar, pbar.T, precision=hi)
    side = 128 // rank
    flat = jnp.concatenate(jnp.split(gram_part, side, axis=0), axis=1)
    sent = jnp.concatenate(
        [
            z_part.reshape(rank, mp, own).transpose(1, 0, 2),
            jnp.broadcast_to(flat, (mp,) + flat.shape),
        ],
        axis=1,
    )
    took = tie(lax.all_to_all(sent, MP, 0, 0, tiled=True), two + [(0, 1), (1, 0)])
    three = fetch(((0, 1), "x", 1), ((1, 0), "y", 1), ((1, -1), "x", -1), ((-1, 1), "y", -1))
    use(two)
    took = jnp.sum(took, axis=0)
    z = took[:rank]
    gram = jnp.concatenate(jnp.split(took[rank:], side, axis=1), axis=0)

    z2 = jnp.concatenate(split(z, 2), axis=0)
    r_local = right_factor(z2, og, r_error)
    low, high = r_local[:half], r_local[half:]
    keep = jnp.where(core == 0, low, high) + other_core(jnp.where(core == 0, high, low))
    r_part = lax.all_to_all(keep.reshape(nz, half // nz, feat), "z", 0, 0, tiled=True)
    r_part = jnp.sum(tie(r_part, three + [(3, 1), (3, 3)], True), axis=0)
    four = fetch(((-1, 1), "x", 1), ((1, 2), "y", 1), ((-1, -1), "y", -1))
    use(three)
    r_part, gram = tie((spread(r_part, MP), gram))
    r_part = jnp.sum(r_part, axis=0) / groups
    lower = jnp.linalg.cholesky(gram)
    inv = jax.scipy.linalg.solve_triangular(lower, jnp.eye(rank, dtype=F32), lower=True)
    mine = tie(spread(r_part, "z"), four, True).reshape(half, feat)
    use(four)
    theirs = other_core(mine)
    r_all = jnp.concatenate([jnp.where(core == 0, mine, theirs), jnp.where(core == 0, theirs, mine)], axis=0)

    q_t = jnp.dot(inv, r_all, precision=hi)
    phat = jnp.dot(inv, pbar, precision=hi)

    mat, pre_grad = state
    ph, pw = split(phat, 2)
    qh, ql = split(q_t, 2)
    left = jnp.concatenate([ph, ph, pw], axis=0).T
    right = jnp.concatenate([qh, ql, qh], axis=0)
    new_error = new_errors(mat, error[:, None], left, right).transpose(1, 0, 2)
    return (pre_grad, new_error, q_t.T)


def solution(mesh):
    sizes = (mesh.shape["replica"] // 2, 2, 4, mesh.shape["mp"] // 4)
    grid = Mesh(mesh.devices.reshape(sizes), ALL)

    def run(*args):
        return shards(sizes, *args)

    return jax.shard_map(
        run,
        mesh=grid,
        in_specs=(
            P(MP, ("z", "core")),
            P(ALL, None),
            P(MP, None),
            P(("z", "core"), MP, None),
            P(),
        ),
        out_specs=(P(MP, ("z", "core")), P(("z", "core"), MP, None), P()),
        check_vma=False,
    )
```

profile of v0, /device:TPU:1, one launch (start us, length us, event | category | flops | bytes accessed | tf_op | source)
XLA Modules:
  0.0 183.8 jit_solution(7824628409264106561)
XLA Ops:
  0.6 3.4 %collective-permute-start = (bf16[4800,128]{1,0:T(8,128)(2,1)}, bf16[4800,128]{1,0:T(8,128)(2,1)}, u32[]{:S(2)}, u32[]{:S(2)}) collective-permute-start(bf16[4800,128]{1,0:T(8,128)(2,1)} %bitcast.58), channel_id=1, source_target_pairs={{1,0},{2,1},{3,2},{0,3},{5,4},{6,5},{7,6},{4,7},{9,8},{10,9},{11,1... | collective-permute-start | bytes 3686408 | tf_op jit(solution)/shard_map/ppermute | solution.py:54
  4.0 2.7 %collective-permute-start.2 = (bf16[4800,128]{1,0:T(8,128)(2,1)}, bf16[4800,128]{1,0:T(8,128)(2,1)}, u32[]{:S(2)}, u32[]{:S(2)}) collective-permute-start(bf16[4800,128]{1,0:T(8,128)(2,1)} %bitcast.60), channel_id=1, source_target_pairs={{4,0},{8,4},{12,8},{0,12},{5,1},{9,5},{13,9},{1,13},{6,2},{10,6},{... | collective-permute-start | bytes 3686408 | tf_op jit(solution)/shard_map/ppermute | solution.py:54
  6.8 1.3 reduce-precision_convert_fusion.2
  8.8 1.7 fusion.27
  11.2 6.4 %all-to-all-start = ((f32[16,32,128]{2,1,0:T(8,128)}), f32[16,32,128]{2,1,0:T(8,128)S(1)}, u32[]{:S(2)}, u32[]{:S(2)}) async-start(f32[16,32,128]{2,1,0:T(8,128)} %broadcast_in_dim.17), calls=%async_computation | async-start | bytes 524288 | tf_op jit(solution)/shard_map/all_to_all | solution.py:45
  17.7 2.3 %fusion.19 = f32[64,150]{1,0:T(8,128)} fusion(f32[1,150,4800]{2,0,1:T(1,128)S(1)} %copy-done, bf16[4800,32]{0,1:T(8,128)(2,1)} %copy-done.15, bf16[4800,32]{0,1:T(8,128)(2,1)S(1)} %get-tuple-element.97), kind=kOutput, calls=%fused_computation.31 | convolution fusion | flops 94828800 | bytes 3532800 | tf_op jit(solution)/shard_map/dot_general | solution.py:35
  20.0 1.3 fusion.2
  21.2 16.3 %all-to-all-done = f32[16,32,128]{2,1,0:T(8,128)S(1)} async-done(((f32[16,32,128]{2,1,0:T(8,128)}), f32[16,32,128]{2,1,0:T(8,128)S(1)}, u32[]{:S(2)}, u32[]{:S(2)}) %all-to-all-start) | async-done | bytes 262176 | tf_op jit(solution)/shard_map/all_to_all | solution.py:45
  39.1 3.0 %collective-permute-start.8 = (bf16[4800,128]{1,0:T(8,128)(2,1)}, bf16[4800,128]{1,0:T(8,128)(2,1)}, u32[]{:S(2)}, u32[]{:S(2)}) collective-permute-start(bf16[4800,128]{1,0:T(8,128)(2,1)} %collective-permute-done.3.refs_4_), channel_id=1, source_target_pairs={{1,0},{2,1},{3,2},{0,3},{5,4},{6,5},{7,6},{4,7},{9,8},{10,9},{11,1... | collective-permute-start | bytes 3686408 | tf_op jit(solution)/shard_map/ppermute | solution.py:54
  42.2 1.7 fusion.23
  44.7 8.2 %all-to-all-start.1 = ((f32[8,32,150]{2,1,0:T(8,128)}), f32[8,32,150]{2,1,0:T(8,128)S(1)}, u32[]{:S(2)}, u32[]{:S(2)}) async-start(f32[8,32,150]{2,1,0:T(8,128)} %broadcast_in_dim.18), calls=%async_computation.1 | async-start | bytes 524288 | tf_op jit(solution)/shard_map/all_to_all | solution.py:45
  52.9 1.4 copy-done.3
  54.3 1.1 copy-done.7
  55.4 1.3 copy-done.11
  56.7 7.5 %shard_map.76 = (f32[150,4800]{1,0:T(8,128)S(1)}, bf16[150,2048]{1,0:T(8,128)(2,1)}) custom-call(s32[5]{0:T(128)S(1)} %stack.69.where, bf16[150,2048]{1,0:T(8,128)(2,1)S(1)} %copy-done.7, bf16[150,4800]{1,0:T(8,128)(2,1)S(1)} %copy-done.3, bf16[4800,128]{1,0:T(8,128)(2,1)S(1)} %bitcast.62, bf16[4800,128]{1,0:T(8,128)(2,1)} %collective-permute-done.refs_1_, ...), custom_call_target="tpu_custom_call" | custom-call | tf_op jit(solution)/shard_map/pallas_call | solution.py:89
  64.2 4.2 %collective-permute-start.4 = (f32[32,150]{1,0:T(8,128)S(1)}, f32[32,150]{1,0:T(8,128)S(1)}, u32[]{:S(2)}, u32[]{:S(2)}) collective-permute-start(f32[32,150]{1,0:T(8,128)S(1)} %reduce_sum.36), channel_id=1, source_target_pairs={{0,16},{16,0},{1,17},{17,1},{2,18},{18,2},{3,19},{19,3},{4,20},{20... | collective-permute-start | bytes 57608 | tf_op jit(solution)/shard_map/ppermute | solution.py:49
  69.5 1.8 fusion.32
  71.5 1.5 fusion.18
  74.0 3.8 %all-to-all-start.2 = ((f32[16,40,128]{2,1,0:T(8,128)}), f32[16,40,128]{2,1,0:T(8,128)S(1)}, u32[]{:S(2)}, u32[]{:S(2)}) async-start(f32[16,40,128]{2,1,0:T(8,128)} %pad_maximum_fusion.2), calls=%async_computation.2 | async-start | bytes 655360 | tf_op jit(solution)/shard_map/all_to_all | solution.py:209
  77.7 2.2 %slice_add_fusion.more_ref = f32[32,4800]{1,0:T(8,128)} fusion(f32[64,4800]{1,0:T(8,128)} %fusion.18), kind=kLoop, calls=%fused_computation.24 | loop fusion | flops 153600 | bytes 1843200 | tf_op jit(solution)/shard_map/add | solution.py:40
  79.9 5.7 %all-to-all-done.2 = f32[16,40,128]{2,1,0:T(8,128)S(1)} async-done(((f32[16,40,128]{2,1,0:T(8,128)}), f32[16,40,128]{2,1,0:T(8,128)S(1)}, u32[]{:S(2)}, u32[]{:S(2)}) %all-to-all-start.2) | async-done | bytes 327712 | tf_op jit(solution)/shard_map/all_to_all | solution.py:209
  85.7 1.3 copy-done.12
  87.0 1.1 copy-done.13
  88.7 4.4 %collective-permute-start.9 = (f32[16,4800]{1,0:T(8,128)S(1)}, f32[16,4800]{1,0:T(8,128)S(1)}, u32[]{:S(2)}, u32[]{:S(2)}) collective-permute-start(f32[16,4800]{1,0:T(8,128)S(1)} %slice_select_fusion), channel_id=1, source_target_pairs={{0,16},{16,0},{1,17},{17,1},{2,18},{18,2},{3,19},{19,3},{4,20},{20... | collective-permute-start | bytes 921608 | tf_op jit(solution)/shard_map/ppermute | solution.py:49
  97.0 8.2 %all-to-all-start.3 = ((f32[8,2,4800]{2,1,0:T(2,128)}), f32[8,2,4800]{2,1,0:T(2,128)S(1)}, u32[]{:S(2)}, u32[]{:S(2)}) async-start(f32[8,2,4800]{2,1,0:T(2,128)} %reshape.30), calls=%async_computation.3 | async-start | bytes 622592 | tf_op jit(solution)/shard_map/all_to_all | solution.py:220
  105.2 1.4 copy-done.4
  106.6 1.1 copy-done.8
  107.7 7.0 %shard_map.78 = (f32[150,4800]{1,0:T(8,128)S(1)}, bf16[150,2048]{1,0:T(8,128)(2,1)}) custom-call(s32[4]{0:T(128)S(1)} %pad_add_fusion.1.where, bf16[150,2048]{1,0:T(8,128)(2,1)S(1)} %copy-done.8, bf16[150,4800]{1,0:T(8,128)(2,1)S(1)} %copy-done.4, bf16[4800,128]{1,0:T(8,128)(2,1)} %collective-permute-done.5.refs_0_, ...), custom_call_target="tpu_custom_call", output_to_operand_aliasing={{0}: (7, {}), {1}: (8, {})} | custom-call | tf_op jit(solution)/shard_map/pallas_call | solution.py:89
  114.7 1.3 all-to-all-done.3
  116.1 5.9 %collective-permute-done.10.refs_0_ = bf16[4800,128]{1,0:T(8,128)(2,1)} collective-permute-done((bf16[4800,128]{1,0:T(8,128)(2,1)}, bf16[4800,128]{1,0:T(8,128)(2,1)}, u32[]{:S(2)}, u32[]{:S(2)}) %collective-permute-start.10) | collective-permute-done | bytes 1228832 | tf_op jit(solution)/shard_map/ppermute | solution.py:54
  122.0 1.8 collective-permute-done.12.refs_2_
  125.4 4.3 %all-to-all-start.4 = ((f32[16,2,4800]{2,1,0:T(2,128)}), f32[16,2,4800]{2,1,0:T(2,128)}, u32[]{:S(2)}, u32[]{:S(2)}) async-start(f32[16,2,4800]{2,1,0:T(2,128)} %broadcast_in_dim.20), calls=%async_computation.4 | async-start | bytes 1245184 | tf_op jit(solution)/shard_map/all_to_all | solution.py:45
  130.3 2.4 %collective-permute-start.14 = (bf16[4800,128]{1,0:T(8,128)(2,1)}, bf16[4800,128]{1,0:T(8,128)(2,1)}, u32[]{:S(2)}, u32[]{:S(2)}) collective-permute-start(bf16[4800,128]{1,0:T(8,128)(2,1)} %collective-permute-done.8.refs_3_), channel_id=1, source_target_pairs={{1,0},{2,1},{3,2},{0,3},{5,4},{6,5},{7,6},{4,7},{9,8},{10,9},{11,1... | collective-permute-start | bytes 3686408 | tf_op jit(solution)/shard_map/ppermute | solution.py:54
  132.7 2.5 %collective-permute-start.15 = (bf16[4800,128]{1,0:T(8,128)(2,1)}, bf16[4800,128]{1,0:T(8,128)(2,1)}, u32[]{:S(2)}, u32[]{:S(2)}) collective-permute-start(bf16[4800,128]{1,0:T(8,128)(2,1)} %collective-permute-done.12.refs_2_), channel_id=1, source_target_pairs={{4,0},{8,4},{12,8},{0,12},{5,1},{9,5},{13,9},{1,13},{6,2},{10,6},{... | collective-permute-start | bytes 3686408 | tf_op jit(solution)/shard_map/ppermute | solution.py:54
  135.2 1.4 copy-done.5
  137.6 7.0 %shard_map.79 = (f32[150,4800]{1,0:T(8,128)S(1)}, bf16[150,2048]{1,0:T(8,128)(2,1)}) custom-call(s32[4]{0:T(128)S(1)} %pad_add_fusion.2.where, bf16[150,2048]{1,0:T(8,128)(2,1)S(1)} %copy-done.9, bf16[150,4800]{1,0:T(8,128)(2,1)S(1)} %copy-done.5, bf16[4800,128]{1,0:T(8,128)(2,1)} %collective-permute-done.10.refs_0_, ...), custom_call_target="tpu_custom_call", output_to_operand_aliasing={{0}: (7, {}), {1}: (8, {})} | custom-call | tf_op jit(solution)/shard_map/pallas_call | solution.py:89
  144.7 1.3 reduce_sum.39
  146.8 8.2 %all-to-all-start.5 = ((f32[8,2,4800]{2,1,0:T(2,128)}), f32[8,2,4800]{2,1,0:T(2,128)S(1)}, u32[]{:S(2)}, u32[]{:S(2)}) async-start(f32[8,2,4800]{2,1,0:T(2,128)} %broadcast_in_dim.21), calls=%async_computation.5 | async-start | bytes 622592 | tf_op jit(solution)/shard_map/all_to_all | solution.py:45
  155.0 2.9 %cholesky.17 = f32[32,32]{1,0:T(8,128)S(1)} custom-call(f32[32,32]{1,0:T(8,128)S(1)} %fusion.38), custom_call_target="Cholesky" | custom-call | tf_op jit(solution)/shard_map/jit(cholesky)/cholesky | solution.py:226
  159.3 2.4 %custom-call.7 = f32[1,32,32]{1,2,0:T(8,128)S(1)} custom-call(f32[1,32,32]{2,1,0:T(8,128)S(1)} %fusion.33), custom_call_target="InvertDiagBlocksLowerTriangular" | custom-call | tf_op jit(solution)/shard_map/jit(_solve_triangular)/triangular_solve | solution.py:227
  162.3 2.6 %all-to-all-done.5 = f32[8,2,4800]{2,1,0:T(2,128)S(1)} async-done(((f32[8,2,4800]{2,1,0:T(2,128)}), f32[8,2,4800]{2,1,0:T(2,128)S(1)}, u32[]{:S(2)}, u32[]{:S(2)}) %all-to-all-start.5) | async-done | bytes 307232 | tf_op jit(solution)/shard_map/all_to_all | solution.py:45
  164.9 1.3 collective-permute-done.15.refs_1_
  166.2 1.2 collective-permute-done.16.refs_2_
  168.3 1.5 collective-permute-start.17
  170.0 1.4 copy-done.6
  172.4 6.2 %shard_map.80 = (f32[150,4800]{1,0:T(8,128)S(1)}, bf16[150,2048]{1,0:T(8,128)(2,1)}) custom-call(s32[3]{0:T(128)S(1)} %pad_add_fusion.where, bf16[150,2048]{1,0:T(8,128)(2,1)S(1)} %copy-done.10, bf16[150,4800]{1,0:T(8,128)(2,1)S(1)} %copy-done.6, bf16[4800,128]{1,0:T(8,128)(2,1)} %collective-permute-done.14.refs_0_, ...), custom_call_target="tpu_custom_call", output_to_operand_aliasing={{0}: (6, {}), {1}: (7, {})} | custom-call | tf_op jit(solution)/shard_map/pallas_call | solution.py:89
  178.7 1.5 fusion.13
  180.8 3.1 %shard_map.81 = f32[150,1,4800]{2,1,0:T(1,128)} custom-call(f32[150,4800]{1,0:T(8,128)S(1)} %get-tuple-element.90.mat_ref, f32[150,1,4800]{2,1,0:T(1,128)S(1)} %bitcast.57, bf16[150,96]{1,0:T(8,128)(2,1)S(1)} %maximum_bitcast_fusion.left_ref, bf16[96,4800]{1,0:T(8,128)(2,1)S(1)} %pad_maximum_fusion.right_ref), custom_call_target="tpu_custom_call" | custom-call | tf_op jit(solution)/shard_map/pallas_call | solution.py:116
  (104 shorter events, 19.6 us)
Async XLA Ops:
  0.6 36.9 %collective-permute-start = (bf16[4800,128]{1,0:T(8,128)(2,1)}, bf16[4800,128]{1,0:T(8,128)(2,1)}, u32[]{:S(2)}, u32[]{:S(2)}) collective-permute-start(bf16[4800,128]{1,0:T(8,128)(2,1)} %bitcast.58), channel_id=1, source_target_pairs={{1,0},{2,1},{3,2},{0,3},{5,4},{6,5},{7,6},{4,7},{9,8},{10,9},{11,1... | collective-permute-start | bytes 3686408 | tf_op jit(solution)/shard_map/ppermute | solution.py:54
  4.0 33.5 %collective-permute-start.1 = (bf16[4800,128]{1,0:T(8,128)(2,1)}, bf16[4800,128]{1,0:T(8,128)(2,1)}, u32[]{:S(2)}, u32[]{:S(2)}) collective-permute-start(bf16[4800,128]{1,0:T(8,128)(2,1)} %bitcast.59), channel_id=1, source_target_pairs={{3,0},{0,1},{1,2},{2,3},{7,4},{4,5},{5,6},{6,7},{11,8},{8,9},{9,10... | collective-permute-start | bytes 3686408 | tf_op jit(solution)/shard_map/ppermute | solution.py:54
  4.0 33.5 %collective-permute-start.2 = (bf16[4800,128]{1,0:T(8,128)(2,1)}, bf16[4800,128]{1,0:T(8,128)(2,1)}, u32[]{:S(2)}, u32[]{:S(2)}) collective-permute-start(bf16[4800,128]{1,0:T(8,128)(2,1)} %bitcast.60), channel_id=1, source_target_pairs={{4,0},{8,4},{12,8},{0,12},{5,1},{9,5},{13,9},{1,13},{6,2},{10,6},{... | collective-permute-start | bytes 3686408 | tf_op jit(solution)/shard_map/ppermute | solution.py:54
  6.8 30.7 %collective-permute-start.3 = (bf16[4800,128]{1,0:T(8,128)(2,1)}, bf16[4800,128]{1,0:T(8,128)(2,1)}, u32[]{:S(2)}, u32[]{:S(2)}) collective-permute-start(bf16[4800,128]{1,0:T(8,128)(2,1)} %bitcast.61), channel_id=1, source_target_pairs={{12,0},{0,4},{4,8},{8,12},{13,1},{1,5},{5,9},{9,13},{14,2},{2,6},{... | collective-permute-start | bytes 3686408 | tf_op jit(solution)/shard_map/ppermute | solution.py:54
  6.8 10.9 %copy-start = (f32[1,150,4800]{2,0,1:T(1,128)S(1)}, f32[1,150,4800]{2,0,1:T(1,128)}, u32[]{:S(2)}) copy-start(f32[1,150,4800]{2,0,1:T(1,128)} %param.8) | copy-start | bytes 8640004
  8.1 0.7 copy-start.15
  11.2 26.3 %all-to-all-start = ((f32[16,32,128]{2,1,0:T(8,128)}), f32[16,32,128]{2,1,0:T(8,128)S(1)}, u32[]{:S(2)}, u32[]{:S(2)}) async-start(f32[16,32,128]{2,1,0:T(8,128)} %broadcast_in_dim.17), calls=%async_computation | async-start | bytes 524288 | tf_op jit(solution)/shard_map/all_to_all | solution.py:45
  17.7 2.3 %copy-start.16 = (bf16[4800,32]{0,1:T(8,128)(2,1)S(1)}, bf16[4800,32]{0,1:T(8,128)(2,1)}, u32[]{:S(2)}) copy-start(bf16[4800,32]{0,1:T(8,128)(2,1)} %copy-done.15) | copy-start | bytes 921604
  37.5 31.8 %collective-permute-start.5 = (bf16[4800,128]{1,0:T(8,128)(2,1)}, bf16[4800,128]{1,0:T(8,128)(2,1)}, u32[]{:S(2)}, u32[]{:S(2)}) collective-permute-start(bf16[4800,128]{1,0:T(8,128)(2,1)} %collective-permute-done.refs_1_), channel_id=1, source_target_pairs={{4,0},{8,4},{12,8},{0,12},{5,1},{9,5},{13,9},{1,13},{6,2},{10,6},{... | collective-permute-start | bytes 3686408 | tf_op jit(solution)/shard_map/ppermute | solution.py:54
  38.6 30.7 %collective-permute-start.7 = (bf16[4800,128]{1,0:T(8,128)(2,1)}, bf16[4800,128]{1,0:T(8,128)(2,1)}, u32[]{:S(2)}, u32[]{:S(2)}) collective-permute-start(bf16[4800,128]{1,0:T(8,128)(2,1)} %collective-permute-done.2.refs_3_), channel_id=1, source_target_pairs={{3,0},{0,1},{1,2},{2,3},{7,4},{4,5},{5,6},{6,7},{11,8},{8,9},{9,10... | collective-permute-start | bytes 3686408 | tf_op jit(solution)/shard_map/ppermute | solution.py:54
  38.6 30.7 %collective-permute-start.6 = (bf16[4800,128]{1,0:T(8,128)(2,1)}, bf16[4800,128]{1,0:T(8,128)(2,1)}, u32[]{:S(2)}, u32[]{:S(2)}) collective-permute-start(bf16[4800,128]{1,0:T(8,128)(2,1)} %collective-permute-done.1.refs_2_), channel_id=1, source_target_pairs={{12,0},{0,4},{4,8},{8,12},{13,1},{1,5},{5,9},{9,13},{14,2},{2,6},{... | collective-permute-start | bytes 3686408 | tf_op jit(solution)/shard_map/ppermute | solution.py:54
  39.1 30.2 %collective-permute-start.8 = (bf16[4800,128]{1,0:T(8,128)(2,1)}, bf16[4800,128]{1,0:T(8,128)(2,1)}, u32[]{:S(2)}, u32[]{:S(2)}) collective-permute-start(bf16[4800,128]{1,0:T(8,128)(2,1)} %collective-permute-done.3.refs_4_), channel_id=1, source_target_pairs={{1,0},{2,1},{3,2},{0,3},{5,4},{6,5},{7,6},{4,7},{9,8},{10,9},{11,1... | collective-permute-start | bytes 3686408 | tf_op jit(solution)/shard_map/ppermute | solution.py:54
  42.2 1.7 copy-start.17
  42.2 1.7 copy-start.18
  44.7 19.5 %all-to-all-start.1 = ((f32[8,32,150]{2,1,0:T(8,128)}), f32[8,32,150]{2,1,0:T(8,128)S(1)}, u32[]{:S(2)}, u32[]{:S(2)}) async-start(f32[8,32,150]{2,1,0:T(8,128)} %broadcast_in_dim.18), calls=%async_computation.1 | async-start | bytes 524288 | tf_op jit(solution)/shard_map/all_to_all | solution.py:45
  52.9 1.4 copy-start.3
  54.3 1.1 copy-start.7
  55.4 1.3 copy-start.11
  64.2 5.0 %collective-permute-start.4 = (f32[32,150]{1,0:T(8,128)S(1)}, f32[32,150]{1,0:T(8,128)S(1)}, u32[]{:S(2)}, u32[]{:S(2)}) collective-permute-start(f32[32,150]{1,0:T(8,128)S(1)} %reduce_sum.36), channel_id=1, source_target_pairs={{0,16},{16,0},{1,17},{17,1},{2,18},{18,2},{3,19},{19,3},{4,20},{20... | collective-permute-start | bytes 57608 | tf_op jit(solution)/shard_map/ppermute | solution.py:49
  69.5 2.0 %copy-start.1 = (f32[1,150,4800]{2,0,1:T(1,128)S(1)}, f32[1,150,4800]{2,0,1:T(1,128)}, u32[]{:S(2)}) copy-start(f32[1,150,4800]{2,0,1:T(1,128)} %param.8) | copy-start | bytes 8640004
  74.0 11.7 %all-to-all-start.2 = ((f32[16,40,128]{2,1,0:T(8,128)}), f32[16,40,128]{2,1,0:T(8,128)S(1)}, u32[]{:S(2)}, u32[]{:S(2)}) async-start(f32[16,40,128]{2,1,0:T(8,128)} %pad_maximum_fusion.2), calls=%async_computation.2 | async-start | bytes 655360 | tf_op jit(solution)/shard_map/all_to_all | solution.py:209
  85.7 1.3 copy-start.12
  87.0 1.1 copy-start.13
  88.7 7.4 %collective-permute-start.9 = (f32[16,4800]{1,0:T(8,128)S(1)}, f32[16,4800]{1,0:T(8,128)S(1)}, u32[]{:S(2)}, u32[]{:S(2)}) collective-permute-start(f32[16,4800]{1,0:T(8,128)S(1)} %slice_select_fusion), channel_id=1, source_target_pairs={{0,16},{16,0},{1,17},{17,1},{2,18},{18,2},{3,19},{19,3},{4,20},{20... | collective-permute-start | bytes 921608 | tf_op jit(solution)/shard_map/ppermute | solution.py:49
  93.1 28.9 %collective-permute-start.10 = (bf16[4800,128]{1,0:T(8,128)(2,1)}, bf16[4800,128]{1,0:T(8,128)(2,1)}, u32[]{:S(2)}, u32[]{:S(2)}) collective-permute-start(bf16[4800,128]{1,0:T(8,128)(2,1)} %collective-permute-done.refs_1_), channel_id=1, source_target_pairs={{1,0},{2,1},{3,2},{0,3},{5,4},{6,5},{7,6},{4,7},{9,8},{10,9},{11,1... | collective-permute-start | bytes 3686408 | tf_op jit(solution)/shard_map/ppermute | solution.py:54
  93.4 28.6 %collective-permute-start.11 = (bf16[4800,128]{1,0:T(8,128)(2,1)}, bf16[4800,128]{1,0:T(8,128)(2,1)}, u32[]{:S(2)}, u32[]{:S(2)}) collective-permute-start(bf16[4800,128]{1,0:T(8,128)(2,1)} %collective-permute-done.2.refs_3_), channel_id=1, source_target_pairs={{4,0},{8,4},{12,8},{0,12},{5,1},{9,5},{13,9},{1,13},{6,2},{10,6},{... | collective-permute-start | bytes 3686408 | tf_op jit(solution)/shard_map/ppermute | solution.py:54
  94.3 29.5 %collective-permute-start.12 = (bf16[4800,128]{1,0:T(8,128)(2,1)}, bf16[4800,128]{1,0:T(8,128)(2,1)}, u32[]{:S(2)}, u32[]{:S(2)}) collective-permute-start(bf16[4800,128]{1,0:T(8,128)(2,1)} %collective-permute-done.7.refs_2_), channel_id=1, source_target_pairs={{3,0},{0,1},{1,2},{2,3},{7,4},{4,5},{5,6},{6,7},{11,8},{8,9},{9,10... | collective-permute-start | bytes 3686408 | tf_op jit(solution)/shard_map/ppermute | solution.py:54
  95.1 29.1 %collective-permute-start.13 = (bf16[4800,128]{1,0:T(8,128)(2,1)}, bf16[4800,128]{1,0:T(8,128)(2,1)}, u32[]{:S(2)}, u32[]{:S(2)}) collective-permute-start(bf16[4800,128]{1,0:T(8,128)(2,1)} %collective-permute-done.8.refs_3_), channel_id=1, source_target_pairs={{12,0},{0,4},{4,8},{8,12},{13,1},{1,5},{5,9},{9,13},{14,2},{2,6},{... | collective-permute-start | bytes 3686408 | tf_op jit(solution)/shard_map/ppermute | solution.py:54
  97.0 19.1 %all-to-all-start.3 = ((f32[8,2,4800]{2,1,0:T(2,128)}), f32[8,2,4800]{2,1,0:T(2,128)S(1)}, u32[]{:S(2)}, u32[]{:S(2)}) async-start(f32[8,2,4800]{2,1,0:T(2,128)} %reshape.30), calls=%async_computation.3 | async-start | bytes 622592 | tf_op jit(solution)/shard_map/all_to_all | solution.py:220
  105.2 1.4 copy-start.4
  106.6 1.1 copy-start.8
  125.4 19.3 %all-to-all-start.4 = ((f32[16,2,4800]{2,1,0:T(2,128)}), f32[16,2,4800]{2,1,0:T(2,128)}, u32[]{:S(2)}, u32[]{:S(2)}) async-start(f32[16,2,4800]{2,1,0:T(2,128)} %broadcast_in_dim.20), calls=%async_computation.4 | async-start | bytes 1245184 | tf_op jit(solution)/shard_map/all_to_all | solution.py:45
  130.3 34.7 %collective-permute-start.14 = (bf16[4800,128]{1,0:T(8,128)(2,1)}, bf16[4800,128]{1,0:T(8,128)(2,1)}, u32[]{:S(2)}, u32[]{:S(2)}) collective-permute-start(bf16[4800,128]{1,0:T(8,128)(2,1)} %collective-permute-done.8.refs_3_), channel_id=1, source_target_pairs={{1,0},{2,1},{3,2},{0,3},{5,4},{6,5},{7,6},{4,7},{9,8},{10,9},{11,1... | collective-permute-start | bytes 3686408 | tf_op jit(solution)/shard_map/ppermute | solution.py:54
  132.7 33.6 %collective-permute-start.15 = (bf16[4800,128]{1,0:T(8,128)(2,1)}, bf16[4800,128]{1,0:T(8,128)(2,1)}, u32[]{:S(2)}, u32[]{:S(2)}) collective-permute-start(bf16[4800,128]{1,0:T(8,128)(2,1)} %collective-permute-done.12.refs_2_), channel_id=1, source_target_pairs={{4,0},{8,4},{12,8},{0,12},{5,1},{9,5},{13,9},{1,13},{6,2},{10,6},{... | collective-permute-start | bytes 3686408 | tf_op jit(solution)/shard_map/ppermute | solution.py:54
  135.1 32.3 %collective-permute-start.16 = (bf16[4800,128]{1,0:T(8,128)(2,1)}, bf16[4800,128]{1,0:T(8,128)(2,1)}, u32[]{:S(2)}, u32[]{:S(2)}) collective-permute-start(bf16[4800,128]{1,0:T(8,128)(2,1)} %collective-permute-done.6.refs_1_), channel_id=1, source_target_pairs={{12,0},{0,4},{4,8},{8,12},{13,1},{1,5},{5,9},{9,13},{14,2},{2,6},{... | collective-permute-start | bytes 3686408 | tf_op jit(solution)/shard_map/ppermute | solution.py:54
  135.2 1.4 copy-start.5
  136.5 1.1 copy-start.9
  146.8 18.2 %all-to-all-start.5 = ((f32[8,2,4800]{2,1,0:T(2,128)}), f32[8,2,4800]{2,1,0:T(2,128)S(1)}, u32[]{:S(2)}, u32[]{:S(2)}) async-start(f32[8,2,4800]{2,1,0:T(2,128)} %broadcast_in_dim.21), calls=%async_computation.5 | async-start | bytes 622592 | tf_op jit(solution)/shard_map/all_to_all | solution.py:45
  168.3 10.3 %collective-permute-start.17 = (f32[16,4800]{1,0:T(8,128)}, f32[16,4800]{1,0:T(8,128)S(1)}, u32[]{:S(2)}, u32[]{:S(2)}) collective-permute-start(f32[16,4800]{1,0:T(8,128)} %reshape.31), channel_id=1, source_target_pairs={{0,16},{16,0},{1,17},{17,1},{2,18},{18,2},{3,19},{19,3},{4,20},{20... | collective-permute-start | bytes 921608 | tf_op jit(solution)/shard_map/ppermute | solution.py:49
  170.0 1.4 copy-start.6
  171.3 1.1 copy-start.10
  172.4 6.2 %copy-start.14 = (f32[16,4800]{1,0:T(8,128)S(1)}, f32[16,4800]{1,0:T(8,128)}, u32[]{:S(2)}) copy-start(f32[16,4800]{1,0:T(8,128)} %reshape.31) | copy-start | bytes 921604
  178.7 2.1 %copy-start.2 = (f32[1,150,4800]{2,0,1:T(1,128)S(1)}, f32[1,150,4800]{2,0,1:T(1,128)}, u32[]{:S(2)}) copy-start(f32[1,150,4800]{2,0,1:T(1,128)} %param.8) | copy-start | bytes 8640004
where the time goes:
time: 185 us; the launch traced here: 184 us
  starting transfers between devices  67.7 us (37%)
  waiting for transfers between devices  37.6 us (20%)
  Pallas kernels  31.4 us (17%)
  local copies, waits for them, and re-layouts  20.6 us (11%)
  other arithmetic  13.2 us (7%)
  matrix products  12.3 us (7%)
    pallas_call x4, Pallas kernels, add_products(): pl.pallas_call(functools.partial(products, n), out_shape=(mat, jax.ShapeD...  27.8 us
    all_to_all x4, starting transfers between devices, spread(): lax.all_to_all(jnp.broadcast_to(x, (n,) + x.shape), axis, 0, 0, tiled=True)  27.1 us
    all_to_all x4, waiting for transfers between devices, spread(): lax.all_to_all(jnp.broadcast_to(x, (n,) + x.shape), axis, 0, 0, tiled=True)  18.9 us
    ppermute x15, starting transfers between devices, shift(): return lax.ppermute(x, axis, [((i + step) % n, i) for i in range(n)])  18.6 us
    unnamed x42, local copies, waits for them, and re-layouts  15.1 us
    ppermute x15, waiting for transfers between devices, shift(): return lax.ppermute(x, axis, [((i + step) % n, i) for i in range(n)])  10.7 us
    dot_general x6, matrix products, dot(): lax.dot_general(a, b, (((ca,), (cb,)), ((), ())), preferred_element_type=...  10.2 us
    ppermute x3, starting transfers between devices, other_core(): return lax.ppermute(x, 'core', [(0, 1), (1, 0)])  10.1 us
  transfers between devices with their start and end apart: 24, of which 10 were waited for; matrix products, arithmetic and copies ran while one was open for 13% of the time, Pallas kernels for 15%

commit v1 on v0

--- a/solution.py
+++ b/solution.py
@@ -54,72 +54,52 @@
     return lax.ppermute(x, axis, [((i + step) % n, i) for i in range(n)])
 
 
-def products(n, where, pre_ref, weight_ref, *refs):
-    blocks, held, (mat_ref, grad_ref, pre_buf, weight_buf, sems) = refs[:n], refs[n:-5], refs[-5:]
-    fetch_pre = pltpu.make_async_copy(pre_ref, pre_buf, sems.at[0])
-    fetch_weight = pltpu.make_async_copy(weight_ref, weight_buf, sems.at[1])
-    fetch_pre.start()
-    fetch_weight.start()
+def products(n, last, where, pre_ref, weight_ref, *refs):
+    blocks, refs = refs[:n], refs[n:]
+    held, (mat_ref, grad_ref) = refs[:-2], refs[-2:]
     if held:
         grad_ref[...] = held[1][...]
+    rows = grad_ref.shape[0]
     own = blocks[0].shape[1]
     spots = [pl.ds(pl.multiple_of(where[i] * own, own), own) for i in range(n)]
-    fetch_pre.wait()
-    pre = jnp.concatenate([pre_buf[:, s] for s in spots], axis=1).astype(F32)
+    pre = jnp.concatenate([pre_ref[:, s] for s in spots], axis=1).astype(F32)
     act, pull = jax.vjp(jax.nn.gelu, pre)
     act = act.astype(BF16)
-    fetch_weight.wait()
-    feat = weight_buf.shape[1]
+    feat = weight_ref.shape[1]
     back = jnp.zeros(pre.shape, F32)
     for lo in range(0, feat, 512):
         part = slice(lo, min(feat, lo + 512))
         piece = jnp.concatenate([b[part, :] for b in blocks], axis=1)
-        back = back + dot(weight_buf[:, part], piece, 1, 0)
+        back = back + dot(weight_ref[:, part], piece, 1, 0)
         more = dot(act, piece, 1, 1)
-        mat_ref[:, part] = more + held[0][:, part] if held else more
+        if held:
+            more = more + held[0][:, part]
+        if last:
+            error_ref, left_ref, right_ref = held[2:]
+            low_rank = dot(left_ref[...], right_ref[:, part], 1, 0)
+            mat_ref[:, 0, part] = more[:rows] + error_ref[:, 0, part] - low_rank
+        else:
+            mat_ref[:, part] = more
     out = pull(back)[0].astype(BF16)
     for i, s in enumerate(spots):
-        grad_ref[:, s] = out[:, i * own:(i + 1) * own]
-
-
-def add_products(where, pre_act, weight, blocks, held):
+        grad_ref[:, s] = out[:rows, i * own:(i + 1) * own]
+
+
+def add_products(where, rows, pre, weight, blocks, held, finish=()):
     vmem = pl.BlockSpec(memory_space=pltpu.VMEM)
     n = len(blocks)
-    mat = jax.ShapeDtypeStruct(weight.shape, F32)
+    mat = (rows, 1, weight.shape[1]) if finish else weight.shape
+    aliases = {n + 4: 1} if held else {}
+    if held and not finish:
+        aliases[n + 3] = 0
     return pl.pallas_call(
-        functools.partial(products, n),
-        out_shape=(mat, jax.ShapeDtypeStruct(pre_act.shape, BF16)),
-        in_specs=[pl.BlockSpec(memory_space=pltpu.SMEM)]
-        + [pl.BlockSpec(memory_space=pltpu.HBM)] * 2
-        + [vmem] * (n + len(held)),
+        functools.partial(products, n, bool(finish)),
+        out_shape=(jax.ShapeDtypeStruct(mat, F32), jax.ShapeDtypeStruct((rows, pre.shape[1]), BF16)),
+        in_specs=[pl.BlockSpec(memory_space=pltpu.SMEM)] + [vmem] * (n + 2 + len(held) + len(finish)),
         out_specs=(vmem, vmem),
-        scratch_shapes=[
-            pltpu.VMEM(pre_act.shape, BF16),
-            pltpu.VMEM(weight.shape, BF16),
-            pltpu.SemaphoreType.DMA((2,)),
-        ],
-        input_output_aliases={n + 3: 0, n + 4: 1} if held else {},
-        compiler_params=pltpu.CompilerParams(vmem_limit_bytes=12 * 2**20),
-    )(where, pre_act, weight, *blocks, *held)
-
-
-def finish(mat_ref, error_ref, left_ref, right_ref, out_ref):
-    feat = mat_ref.shape[1]
-    left = left_ref[...]
-    for lo in range(0, feat, 512):
-        part = slice(lo, min(feat, lo + 512))
-        out_ref[:, 0, part] = mat_ref[:, part] + error_ref[:, 0, part] - dot(left, right_ref[:, part], 1, 0)
-
-
-def new_errors(mat, error, left, right):
-    vmem = pl.BlockSpec(memory_space=pltpu.VMEM)
-    return pl.pallas_call(
-        finish,
-        out_shape=jax.ShapeDtypeStruct(error.shape, F32),
-        in_specs=[vmem] * 4,
-        out_specs=vmem,
-        compiler_params=pltpu.CompilerParams(vmem_limit_bytes=12 * 2**20),
-    )(mat, error, left, right)
+        input_output_aliases=aliases,
+        compiler_params=pltpu.CompilerParams(vmem_limit_bytes=14 * 2**20),
+    )(where, pre, weight, *blocks, *held, *finish)
 
 
 def right_rows(z_ref, og_ref, more_ref, out_ref):
@@ -173,9 +153,12 @@
             state[:] = out[2]
         return out[0]
 
-    def use(keys):
+    pad = ((0, -hid % 16), (0, 0))
+    pre_pad, w_pad = jnp.pad(pre_act, pad), jnp.pad(weight, pad)
+
+    def use(keys, finish=()):
         where = jnp.stack([((iy + dy) & (ny - 1)) * nx + ((ix + dx) & (nx - 1)) for dy, dx in keys])
-        state[:] = add_products(where, pre_act, weight, [got[k] for k in keys], state)
+        state[:] = add_products(where, hid, pre_pad, w_pad, [got[k] for k in keys], state, finish)
 
     one = fetch(((0, 0), "x", 1), ((0, 0), "x", -1), ((0, 0), "y", 1), ((0, 0), "y", -1))
 
@@ -208,7 +191,6 @@
     )
     took = tie(lax.all_to_all(sent, MP, 0, 0, tiled=True), two + [(0, 1), (1, 0)])
     three = fetch(((0, 1), "x", 1), ((1, 0), "y", 1), ((1, -1), "x", -1), ((-1, 1), "y", -1))
-    use(two)
     took = jnp.sum(took, axis=0)
     z = took[:rank]
     gram = jnp.concatenate(jnp.split(took[rank:], side, axis=1), axis=0)
@@ -217,28 +199,32 @@
     r_local = right_factor(z2, og, r_error)
     low, high = r_local[:half], r_local[half:]
     keep = jnp.where(core == 0, low, high) + other_core(jnp.where(core == 0, high, low))
-    r_part = lax.all_to_all(keep.reshape(nz, half // nz, feat), "z", 0, 0, tiled=True)
-    r_part = jnp.sum(tie(r_part, three + [(3, 1), (3, 3)], True), axis=0)
-    four = fetch(((-1, 1), "x", 1), ((1, 2), "y", 1), ((-1, -1), "y", -1))
-    use(three)
-    r_part, gram = tie((spread(r_part, MP), gram))
-    r_part = jnp.sum(r_part, axis=0) / groups
+    keep = tie(keep, two, True)
+    use(two)
+    gram = tie(gram, [], True)
     lower = jnp.linalg.cholesky(gram)
     inv = jax.scipy.linalg.solve_triangular(lower, jnp.eye(rank, dtype=F32), lower=True)
+    r_part = lax.all_to_all(keep.reshape(nz, half // nz, feat), "z", 0, 0, tiled=True)
+    r_part, inv = tie((r_part, inv), three + [(3, 1), (3, 3)], True)
+    r_part = jnp.sum(r_part, axis=0)
+    four = fetch(((-1, 1), "x", 1), ((1, 2), "y", 1), ((-1, -1), "y", -1))
+    r_part = tie(spread(r_part, MP), [], True)
+    use(three)
+    r_part = jnp.sum(r_part, axis=0) / groups
     mine = tie(spread(r_part, "z"), four, True).reshape(half, feat)
-    use(four)
     theirs = other_core(mine)
     r_all = jnp.concatenate([jnp.where(core == 0, mine, theirs), jnp.where(core == 0, theirs, mine)], axis=0)
 
     q_t = jnp.dot(inv, r_all, precision=hi)
     phat = jnp.dot(inv, pbar, precision=hi)
 
-    mat, pre_grad = state
     ph, pw = split(phat, 2)
     qh, ql = split(q_t, 2)
     left = jnp.concatenate([ph, ph, pw], axis=0).T
     right = jnp.concatenate([qh, ql, qh], axis=0)
-    new_error = new_errors(mat, error[:, None], left, right).transpose(1, 0, 2)
+    use(four, (error[:, None], left, right))
+    new_error, pre_grad = state
+    new_error = new_error.transpose(1, 0, 2)
     return (pre_grad, new_error, q_t.T)
 
 

time: 185 us -> 192 us (1.038)
  waiting for transfers between devices: 37.6 us -> 46.6 us
  Pallas kernels: 31.4 us -> 26.3 us
  local copies, waits for them, and re-layouts: 20.6 us -> 24.1 us
  other arithmetic: 13.2 us -> 15.7 us
    all_to_all x1, waiting for transfers between devices: 1.34 us -> 6.95 us  [shards(): lax.all_to_all(keep.reshape(nz, half // nz, feat), 'z', 0, 0, tiled=True)]
    pallas_call x5 -> x4, Pallas kernels: 30.9 us -> 25.8 us  [add_products(): pl.pallas_call(functools.partial(products, n, bool(finish)), out_shape=(j...]
    all_to_all x4, waiting for transfers between devices: 18.9 us -> 23.5 us  [spread(): lax.all_to_all(jnp.broadcast_to(x, (n,) + x.shape), axis, 0, 0, tiled=True)]
    all_to_all x4, starting transfers between devices: 27.1 us -> 23.7 us  [spread(): lax.all_to_all(jnp.broadcast_to(x, (n,) + x.shape), axis, 0, 0, tiled=True)]
    ppermute x15, waiting for transfers between devices: 10.7 us -> 8.34 us  [shift(): return lax.ppermute(x, axis, [((i + step) % n, i) for i in range(n)])]
    dot_general x6, matrix products: 10.2 us -> 8.17 us  [dot(): lax.dot_general(a, b, (((ca,), (cb,)), ((), ())), preferred_element_type=...]
    unnamed x42 -> x28, local copies, waits for them, and re-layouts: 15.1 us -> 13.9 us
  transfers between devices with their start and end apart: 24 -> 24, of which waited for: 10 -> 9; matrix products, arithmetic and copies ran while one was open for 13% -> 14% of each run, Pallas kernels for 15% -> 10%
where the time goes in v1:
time: 192 us; the launch traced here: 191 us
  starting transfers between devices  66.2 us (34%)
  waiting for transfers between devices  46.6 us (24%)
  Pallas kernels  26.3 us (14%)
  local copies, waits for them, and re-layouts  24.1 us (13%)
  other arithmetic  15.7 us (8%)
  matrix products  10.8 us (6%)
    pallas_call x4, Pallas kernels, add_products(): pl.pallas_call(functools.partial(products, n, bool(finish)), out_shape=(j...  25.8 us
    all_to_all x4, starting transfers between devices, spread(): lax.all_to_all(jnp.broadcast_to(x, (n,) + x.shape), axis, 0, 0, tiled=True)  23.7 us
    all_to_all x4, waiting for transfers between devices, spread(): lax.all_to_all(jnp.broadcast_to(x, (n,) + x.shape), axis, 0, 0, tiled=True)  23.5 us
    ppermute x15, starting transfers between devices, shift(): return lax.ppermute(x, axis, [((i + step) % n, i) for i in range(n)])  18.6 us
    unnamed x28, local copies, waits for them, and re-layouts  13.9 us
    ppermute x3, starting transfers between devices, other_core(): return lax.ppermute(x, 'core', [(0, 1), (1, 0)])  11.9 us
    ppermute x15, waiting for transfers between devices, shift(): return lax.ppermute(x, axis, [((i + step) % n, i) for i in range(n)])  8.34 us
    all_to_all x1, starting transfers between devices, shards(): lax.all_to_all(keep.reshape(nz, half // nz, feat), 'z', 0, 0, tiled=True)  8.18 us
  transfers between devices with their start and end apart: 24, of which 9 were waited for; matrix products, arithmetic and copies ran while one was open for 14% of the time, Pallas kernels for 10%

profile of v1, /device:TPU:1, one launch (start us, length us, event | category | flops | bytes accessed | tf_op | source)
XLA Modules:
  0.0 190.7 jit_solution(4886990264168630103)
XLA Ops:
  0.6 3.4 %collective-permute-start = (bf16[4800,128]{1,0:T(8,128)(2,1)}, bf16[4800,128]{1,0:T(8,128)(2,1)}, u32[]{:S(2)}, u32[]{:S(2)}) collective-permute-start(bf16[4800,128]{1,0:T(8,128)(2,1)} %bitcast.58), channel_id=1, source_target_pairs={{1,0},{2,1},{3,2},{0,3},{5,4},{6,5},{7,6},{4,7},{9,8},{10,9},{11,1... | collective-permute-start | bytes 3686408 | tf_op jit(solution)/shard_map/ppermute | solution.py:54
  4.0 2.7 %collective-permute-start.2 = (bf16[4800,128]{1,0:T(8,128)(2,1)}, bf16[4800,128]{1,0:T(8,128)(2,1)}, u32[]{:S(2)}, u32[]{:S(2)}) collective-permute-start(bf16[4800,128]{1,0:T(8,128)(2,1)} %bitcast.60), channel_id=1, source_target_pairs={{4,0},{8,4},{12,8},{0,12},{5,1},{9,5},{13,9},{1,13},{6,2},{10,6},{... | collective-permute-start | bytes 3686408 | tf_op jit(solution)/shard_map/ppermute | solution.py:54
  6.8 1.1 reduce-precision_convert_fusion.2
  9.1 6.4 %all-to-all-start = ((f32[16,32,128]{2,1,0:T(8,128)}), f32[16,32,128]{2,1,0:T(8,128)S(1)}, u32[]{:S(2)}, u32[]{:S(2)}) async-start(f32[16,32,128]{2,1,0:T(8,128)} %broadcast_in_dim.17), calls=%async_computation | async-start | bytes 524288 | tf_op jit(solution)/shard_map/all_to_all | solution.py:45
  15.5 2.6 %fusion.19 = f32[64,150]{1,0:T(8,128)S(1)} fusion(f32[1,150,4800]{2,0,1:T(1,128)} %param.8, bf16[4800,32]{0,1:T(8,128)(2,1)S(1)} %get-tuple-element.122, bf16[4800,32]{0,1:T(8,128)(2,1)S(1)} %get-tuple-element.121), kind=kOutput, calls=%fused_computation.31 | convolution fusion | flops 94828800 | bytes 3532800 | tf_op jit(solution)/shard_map/dot_general | solution.py:35
  18.8 18.7 %all-to-all-done = f32[16,32,128]{2,1,0:T(8,128)S(1)} async-done(((f32[16,32,128]{2,1,0:T(8,128)}), f32[16,32,128]{2,1,0:T(8,128)S(1)}, u32[]{:S(2)}, u32[]{:S(2)}) %all-to-all-start) | async-done | bytes 262176 | tf_op jit(solution)/shard_map/all_to_all | solution.py:45
  37.5 1.1 collective-permute-start.5
  39.2 3.0 %collective-permute-start.8 = (bf16[4800,128]{1,0:T(8,128)(2,1)}, bf16[4800,128]{1,0:T(8,128)(2,1)}, u32[]{:S(2)}, u32[]{:S(2)}) collective-permute-start(bf16[4800,128]{1,0:T(8,128)(2,1)} %collective-permute-done.3.refs_4_), channel_id=1, source_target_pairs={{1,0},{2,1},{3,2},{0,3},{5,4},{6,5},{7,6},{4,7},{9,8},{10,9},{11,1... | collective-permute-start | bytes 3686408 | tf_op jit(solution)/shard_map/ppermute | solution.py:54
  43.5 8.2 %all-to-all-start.1 = ((f32[8,32,150]{2,1,0:T(8,128)}), f32[8,32,150]{2,1,0:T(8,128)}, u32[]{:S(2)}, u32[]{:S(2)}) async-start(f32[8,32,150]{2,1,0:T(8,128)} %broadcast_in_dim.18), calls=%async_computation.1 | async-start | bytes 524288 | tf_op jit(solution)/shard_map/all_to_all | solution.py:45
  51.8 1.5 pad.9.weight_ref
  53.4 6.7 %shard_map.76 = (f32[160,4800]{1,0:T(8,128)S(1)}, bf16[150,2048]{1,0:T(8,128)(2,1)}) custom-call(s32[5]{0:T(128)S(1)} %stack.69.where, bf16[160,2048]{1,0:T(8,128)(2,1)S(1)} %pad.8.pre_ref, bf16[160,4800]{1,0:T(8,128)(2,1)S(1)} %pad.9.weight_ref, bf16[4800,128]{1,0:T(8,128)(2,1)S(1)} %bitcast.62, bf16[4800,128]{1,0:T(8,128)(2,1)} %collective-permute-done.refs_1_, ...), custom_call_target="tpu_custom_call" | custom-call | tf_op jit(solution)/shard_map/pallas_call | solution.py:95
  60.0 1.6 copy-done
  61.7 1.0 reduce_sum.36
  62.6 4.8 %collective-permute-start.4 = (f32[32,150]{1,0:T(8,128)S(1)}, f32[32,150]{1,0:T(8,128)S(1)}, u32[]{:S(2)}, u32[]{:S(2)}) collective-permute-start(f32[32,150]{1,0:T(8,128)S(1)} %reduce_sum.36), channel_id=1, source_target_pairs={{0,16},{16,0},{1,17},{17,1},{2,18},{18,2},{3,19},{19,3},{4,20},{20... | collective-permute-start | bytes 57608 | tf_op jit(solution)/shard_map/ppermute | solution.py:49
  68.4 3.4 %fusion.18 = f32[64,4800]{1,0:T(8,128)} fusion(f32[1,150,4800]{2,0,1:T(1,128)} %param.8, bf16[32,150]{1,0:T(8,128)(2,1)S(1)} %get-tuple-element.128, bf16[32,150]{1,0:T(8,128)(2,1)S(1)} %get-tuple-element.127), kind=kOutput, calls=%fused_computation.30 | convolution fusion | flops 93638400 | bytes 4128000 | tf_op jit(solution)/shard_map/dot_general | solution.py:35
  73.5 3.8 %all-to-all-start.2 = ((f32[16,40,128]{2,1,0:T(8,128)}), f32[16,40,128]{2,1,0:T(8,128)S(1)}, u32[]{:S(2)}, u32[]{:S(2)}) async-start(f32[16,40,128]{2,1,0:T(8,128)} %pad_maximum_fusion.2), calls=%async_computation.2 | async-start | bytes 655360 | tf_op jit(solution)/shard_map/all_to_all | solution.py:192
  77.3 1.3 slice_add_fusion.more_ref
  78.6 6.6 %all-to-all-done.2 = f32[16,40,128]{2,1,0:T(8,128)S(1)} async-done(((f32[16,40,128]{2,1,0:T(8,128)}), f32[16,40,128]{2,1,0:T(8,128)S(1)}, u32[]{:S(2)}, u32[]{:S(2)}) %all-to-all-start.2) | async-done | bytes 327712 | tf_op jit(solution)/shard_map/all_to_all | solution.py:192
  85.2 1.3 copy-done.9
  87.1 5.4 %collective-permute-start.9 = (f32[16,4800]{1,0:T(8,128)S(1)}, f32[16,4800]{1,0:T(8,128)S(1)}, u32[]{:S(2)}, u32[]{:S(2)}) collective-permute-start(f32[16,4800]{1,0:T(8,128)S(1)} %slice_select_fusion), channel_id=1, source_target_pairs={{0,16},{16,0},{1,17},{17,1},{2,18},{18,2},{3,19},{19,3},{4,20},{20... | collective-permute-start | bytes 921608 | tf_op jit(solution)/shard_map/ppermute | solution.py:49
  97.9 1.9 copy-done.1
  99.7 6.2 %shard_map.78 = (f32[160,4800]{1,0:T(8,128)S(1)}, bf16[150,2048]{1,0:T(8,128)(2,1)}) custom-call(s32[4]{0:T(128)S(1)} %pad_add_fusion.1.where, bf16[160,2048]{1,0:T(8,128)(2,1)S(1)} %pad.8.pre_ref, bf16[160,4800]{1,0:T(8,128)(2,1)S(1)} %pad.9.weight_ref, ...), custom_call_target="tpu_custom_call", output_to_operand_aliasing={{1}: (8, {}), {0}: (7, {})} | custom-call | tf_op jit(solution)/shard_map/pallas_call | solution.py:95
  105.9 1.6 copy-done.2
  107.6 2.9 %cholesky.17 = f32[32,32]{1,0:T(8,128)S(1)} custom-call(f32[32,32]{1,0:T(8,128)S(1)} %fusion.38), custom_call_target="Cholesky" | custom-call | tf_op jit(solution)/shard_map/jit(cholesky)/cholesky | solution.py:205
  110.6 0.9 reshape.30
  111.5 8.2 %all-to-all-start.3 = ((f32[8,2,4800]{2,1,0:T(2,128)}), f32[8,2,4800]{2,1,0:T(2,128)S(1)}, u32[]{:S(2)}, u32[]{:S(2)}) async-start(f32[8,2,4800]{2,1,0:T(2,128)} %reshape.30), calls=%async_computation.3 | async-start | bytes 622592 | tf_op jit(solution)/shard_map/all_to_all | solution.py:207
  121.0 2.4 %custom-call.7 = f32[1,32,32]{1,2,0:T(8,128)S(1)} custom-call(f32[1,32,32]{2,1,0:T(8,128)S(1)} %fusion.33), custom_call_target="InvertDiagBlocksLowerTriangular" | custom-call | tf_op jit(solution)/shard_map/jit(_solve_triangular)/triangular_solve | solution.py:206
  123.6 7.0 %all-to-all-done.3 = f32[8,2,4800]{2,1,0:T(2,128)S(1)} async-done(((f32[8,2,4800]{2,1,0:T(2,128)}), f32[8,2,4800]{2,1,0:T(2,128)S(1)}, u32[]{:S(2)}, u32[]{:S(2)}) %all-to-all-start.3) | async-done | bytes 307232 | tf_op jit(solution)/shard_map/all_to_all | solution.py:207
  130.7 1.0 broadcast_in_dim.20
  131.7 4.7 %all-to-all-start.4 = ((f32[16,2,4800]{2,1,0:T(2,128)}), f32[16,2,4800]{2,1,0:T(2,128)}, u32[]{:S(2)}, u32[]{:S(2)}) async-start(f32[16,2,4800]{2,1,0:T(2,128)} %broadcast_in_dim.20), calls=%async_computation.4 | async-start | bytes 1245184 | tf_op jit(solution)/shard_map/all_to_all | solution.py:45
  136.5 2.5 %collective-permute-start.14 = (bf16[4800,128]{1,0:T(8,128)(2,1)}, bf16[4800,128]{1,0:T(8,128)(2,1)S(1)}, u32[]{:S(2)}, u32[]{:S(2)}) collective-permute-start(bf16[4800,128]{1,0:T(8,128)(2,1)} %collective-permute-done.8.refs_3_), channel_id=1, source_target_pairs={{1,0},{2,1},{3,2},{0,3},{5,4},{6,5},{7,6},{4,7},{9,8},{10,9},{11,1... | collective-permute-start | bytes 3686408 | tf_op jit(solution)/shard_map/ppermute | solution.py:54
  139.0 2.4 %collective-permute-start.15 = (bf16[4800,128]{1,0:T(8,128)(2,1)}, bf16[4800,128]{1,0:T(8,128)(2,1)}, u32[]{:S(2)}, u32[]{:S(2)}) collective-permute-start(bf16[4800,128]{1,0:T(8,128)(2,1)} %collective-permute-done.12.refs_2_), channel_id=1, source_target_pairs={{4,0},{8,4},{12,8},{0,12},{5,1},{9,5},{13,9},{1,13},{6,2},{10,6},{... | collective-permute-start | bytes 3686408 | tf_op jit(solution)/shard_map/ppermute | solution.py:54
  141.4 4.8 %all-to-all-done.4 = f32[16,2,4800]{2,1,0:T(2,128)} async-done(((f32[16,2,4800]{2,1,0:T(2,128)}), f32[16,2,4800]{2,1,0:T(2,128)}, u32[]{:S(2)}, u32[]{:S(2)}) %all-to-all-start.4) | async-done | bytes 614432 | tf_op jit(solution)/shard_map/all_to_all | solution.py:45
  146.2 1.3 reduce_sum.39
  148.4 4.4 %all-to-all-start.5 = ((f32[8,2,4800]{2,1,0:T(2,128)}), f32[8,2,4800]{2,1,0:T(2,128)}, u32[]{:S(2)}, u32[]{:S(2)}) async-start(f32[8,2,4800]{2,1,0:T(2,128)} %broadcast_in_dim.21), calls=%async_computation.5 | async-start | bytes 622592 | tf_op jit(solution)/shard_map/all_to_all | solution.py:45
  154.5 1.5 copy.40
  156.0 1.9 copy-done.3
  157.9 6.2 %shard_map.79 = (f32[160,4800]{1,0:T(8,128)S(1)}, bf16[150,2048]{1,0:T(8,128)(2,1)}) custom-call(s32[4]{0:T(128)S(1)} %pad_add_fusion.2.where, bf16[160,2048]{1,0:T(8,128)(2,1)S(1)} %pad.8.pre_ref, bf16[160,4800]{1,0:T(8,128)(2,1)S(1)} %pad.9.weight_ref, ...), custom_call_target="tpu_custom_call", output_to_operand_aliasing={{1}: (8, {}), {0}: (7, {})} | custom-call | tf_op jit(solution)/shard_map/pallas_call | solution.py:95
  164.1 1.6 copy-done.4
  165.7 3.0 %collective-permute-done.14.refs_0_ = bf16[4800,128]{1,0:T(8,128)(2,1)S(1)} collective-permute-done((bf16[4800,128]{1,0:T(8,128)(2,1)}, bf16[4800,128]{1,0:T(8,128)(2,1)S(1)}, u32[]{:S(2)}, u32[]{:S(2)}) %collective-permute-start.14) | collective-permute-done | bytes 1228832 | tf_op jit(solution)/shard_map/ppermute | solution.py:54
  168.7 4.4 %collective-permute-done.15.refs_1_ = bf16[4800,128]{1,0:T(8,128)(2,1)} collective-permute-done((bf16[4800,128]{1,0:T(8,128)(2,1)}, bf16[4800,128]{1,0:T(8,128)(2,1)}, u32[]{:S(2)}, u32[]{:S(2)}) %collective-permute-start.15) | collective-permute-done | bytes 1228832 | tf_op jit(solution)/shard_map/ppermute | solution.py:54
  173.1 0.9 collective-permute-done.16.refs_2_
  174.0 1.9 reshape.31
  175.9 1.7 collective-permute-start.17
  179.0 1.0 broadcast_select_fusion.1
  180.1 1.5 fusion.13
  182.2 1.8 copy-done.7
  184.0 6.7 %shard_map.80 = (f32[150,1,4800]{2,1,0:T(1,128)}, bf16[150,2048]{1,0:T(8,128)(2,1)}) custom-call(s32[3]{0:T(128)S(1)} %pad_add_fusion.where, bf16[160,2048]{1,0:T(8,128)(2,1)S(1)} %pad.8.pre_ref, bf16[160,4800]{1,0:T(8,128)(2,1)S(1)} %pad.9.weight_ref, bf16[4800,128]{1,0:T(8,128)(2,1)S(1)} %collective-permute-done.14.refs_0_, ...), custom_call_target="tpu_custom_call", output_to_operand_aliasing={{1}: (7, {})} | custom-call | tf_op jit(solution)/shard_map/pallas_call | solution.py:95
  (91 shorter events, 18.8 us)
Async XLA Ops:
  0.6 7.3 %copy-start.8 = (bf16[128,4800]{0,1:T(8,128)(2,1)S(1)}, bf16[128,4800]{0,1:T(8,128)(2,1)}, u32[]{:S(2)}) copy-start(bf16[128,4800]{0,1:T(8,128)(2,1)} %param.6) | copy-start | bytes 3686404
  0.6 36.9 %collective-permute-start = (bf16[4800,128]{1,0:T(8,128)(2,1)}, bf16[4800,128]{1,0:T(8,128)(2,1)}, u32[]{:S(2)}, u32[]{:S(2)}) collective-permute-start(bf16[4800,128]{1,0:T(8,128)(2,1)} %bitcast.58), channel_id=1, source_target_pairs={{1,0},{2,1},{3,2},{0,3},{5,4},{6,5},{7,6},{4,7},{9,8},{10,9},{11,1... | collective-permute-start | bytes 3686408 | tf_op jit(solution)/shard_map/ppermute | solution.py:54
  4.0 33.5 %collective-permute-start.1 = (bf16[4800,128]{1,0:T(8,128)(2,1)}, bf16[4800,128]{1,0:T(8,128)(2,1)}, u32[]{:S(2)}, u32[]{:S(2)}) collective-permute-start(bf16[4800,128]{1,0:T(8,128)(2,1)} %bitcast.59), channel_id=1, source_target_pairs={{3,0},{0,1},{1,2},{2,3},{7,4},{4,5},{5,6},{6,7},{11,8},{8,9},{9,10... | collective-permute-start | bytes 3686408 | tf_op jit(solution)/shard_map/ppermute | solution.py:54
  4.0 33.5 %collective-permute-start.2 = (bf16[4800,128]{1,0:T(8,128)(2,1)}, bf16[4800,128]{1,0:T(8,128)(2,1)}, u32[]{:S(2)}, u32[]{:S(2)}) collective-permute-start(bf16[4800,128]{1,0:T(8,128)(2,1)} %bitcast.60), channel_id=1, source_target_pairs={{4,0},{8,4},{12,8},{0,12},{5,1},{9,5},{13,9},{1,13},{6,2},{10,6},{... | collective-permute-start | bytes 3686408 | tf_op jit(solution)/shard_map/ppermute | solution.py:54
  6.8 30.7 %collective-permute-start.3 = (bf16[4800,128]{1,0:T(8,128)(2,1)}, bf16[4800,128]{1,0:T(8,128)(2,1)}, u32[]{:S(2)}, u32[]{:S(2)}) collective-permute-start(bf16[4800,128]{1,0:T(8,128)(2,1)} %bitcast.61), channel_id=1, source_target_pairs={{12,0},{0,4},{4,8},{8,12},{13,1},{1,5},{5,9},{9,13},{14,2},{2,6},{... | collective-permute-start | bytes 3686408 | tf_op jit(solution)/shard_map/ppermute | solution.py:54
  9.1 28.4 %all-to-all-start = ((f32[16,32,128]{2,1,0:T(8,128)}), f32[16,32,128]{2,1,0:T(8,128)S(1)}, u32[]{:S(2)}, u32[]{:S(2)}) async-start(f32[16,32,128]{2,1,0:T(8,128)} %broadcast_in_dim.17), calls=%async_computation | async-start | bytes 524288 | tf_op jit(solution)/shard_map/all_to_all | solution.py:45
  15.5 2.7 %copy-start.6 = (f32[1,150,4800]{2,0,1:T(1,128)S(1)}, f32[1,150,4800]{2,0,1:T(1,128)}, u32[]{:S(2)}) copy-start(f32[1,150,4800]{2,0,1:T(1,128)} %param.8) | copy-start | bytes 8640004
  18.2 24.0 %copy-start.10 = (bf16[150,2048]{1,0:T(8,128)(2,1)S(1)}, bf16[150,2048]{1,0:T(8,128)(2,1)}, u32[]{:S(2)}) copy-start(bf16[150,2048]{1,0:T(8,128)(2,1)} %param.5) | copy-start | bytes 1843204
  37.5 30.8 %collective-permute-start.5 = (bf16[4800,128]{1,0:T(8,128)(2,1)}, bf16[4800,128]{1,0:T(8,128)(2,1)}, u32[]{:S(2)}, u32[]{:S(2)}) collective-permute-start(bf16[4800,128]{1,0:T(8,128)(2,1)} %collective-permute-done.refs_1_), channel_id=1, source_target_pairs={{4,0},{8,4},{12,8},{0,12},{5,1},{9,5},{13,9},{1,13},{6,2},{10,6},{... | collective-permute-start | bytes 3686408 | tf_op jit(solution)/shard_map/ppermute | solution.py:54
  38.6 29.7 %collective-permute-start.7 = (bf16[4800,128]{1,0:T(8,128)(2,1)}, bf16[4800,128]{1,0:T(8,128)(2,1)}, u32[]{:S(2)}, u32[]{:S(2)}) collective-permute-start(bf16[4800,128]{1,0:T(8,128)(2,1)} %collective-permute-done.2.refs_3_), channel_id=1, source_target_pairs={{3,0},{0,1},{1,2},{2,3},{7,4},{4,5},{5,6},{6,7},{11,8},{8,9},{9,10... | collective-permute-start | bytes 3686408 | tf_op jit(solution)/shard_map/ppermute | solution.py:54
  38.6 29.8 %collective-permute-start.6 = (bf16[4800,128]{1,0:T(8,128)(2,1)}, bf16[4800,128]{1,0:T(8,128)(2,1)}, u32[]{:S(2)}, u32[]{:S(2)}) collective-permute-start(bf16[4800,128]{1,0:T(8,128)(2,1)} %collective-permute-done.1.refs_2_), channel_id=1, source_target_pairs={{12,0},{0,4},{4,8},{8,12},{13,1},{1,5},{5,9},{9,13},{14,2},{2,6},{... | collective-permute-start | bytes 3686408 | tf_op jit(solution)/shard_map/ppermute | solution.py:54
  39.2 29.2 %collective-permute-start.8 = (bf16[4800,128]{1,0:T(8,128)(2,1)}, bf16[4800,128]{1,0:T(8,128)(2,1)}, u32[]{:S(2)}, u32[]{:S(2)}) collective-permute-start(bf16[4800,128]{1,0:T(8,128)(2,1)} %collective-permute-done.3.refs_4_), channel_id=1, source_target_pairs={{1,0},{2,1},{3,2},{0,3},{5,4},{6,5},{7,6},{4,7},{9,8},{10,9},{11,1... | collective-permute-start | bytes 3686408 | tf_op jit(solution)/shard_map/ppermute | solution.py:54
  43.5 18.1 %all-to-all-start.1 = ((f32[8,32,150]{2,1,0:T(8,128)}), f32[8,32,150]{2,1,0:T(8,128)}, u32[]{:S(2)}, u32[]{:S(2)}) async-start(f32[8,32,150]{2,1,0:T(8,128)} %broadcast_in_dim.18), calls=%async_computation.1 | async-start | bytes 524288 | tf_op jit(solution)/shard_map/all_to_all | solution.py:45
  60.0 1.6 copy-start
  62.6 5.7 %collective-permute-start.4 = (f32[32,150]{1,0:T(8,128)S(1)}, f32[32,150]{1,0:T(8,128)S(1)}, u32[]{:S(2)}, u32[]{:S(2)}) collective-permute-start(f32[32,150]{1,0:T(8,128)S(1)} %reduce_sum.36), channel_id=1, source_target_pairs={{0,16},{16,0},{1,17},{17,1},{2,18},{18,2},{3,19},{19,3},{4,20},{20... | collective-permute-start | bytes 57608 | tf_op jit(solution)/shard_map/ppermute | solution.py:49
  68.4 3.4 %copy-start.11 = (bf16[150,2048]{1,0:T(8,128)(2,1)S(1)}, bf16[150,2048]{1,0:T(8,128)(2,1)}, u32[]{:S(2)}) copy-start(bf16[150,2048]{1,0:T(8,128)(2,1)} %param.5) | copy-start | bytes 1843204
  73.5 11.7 %all-to-all-start.2 = ((f32[16,40,128]{2,1,0:T(8,128)}), f32[16,40,128]{2,1,0:T(8,128)S(1)}, u32[]{:S(2)}, u32[]{:S(2)}) async-start(f32[16,40,128]{2,1,0:T(8,128)} %pad_maximum_fusion.2), calls=%async_computation.2 | async-start | bytes 655360 | tf_op jit(solution)/shard_map/all_to_all | solution.py:192
  85.2 1.3 copy-start.9
  87.1 10.7 %collective-permute-start.9 = (f32[16,4800]{1,0:T(8,128)S(1)}, f32[16,4800]{1,0:T(8,128)S(1)}, u32[]{:S(2)}, u32[]{:S(2)}) collective-permute-start(f32[16,4800]{1,0:T(8,128)S(1)} %slice_select_fusion), channel_id=1, source_target_pairs={{0,16},{16,0},{1,17},{17,1},{2,18},{18,2},{3,19},{19,3},{4,20},{20... | collective-permute-start | bytes 921608 | tf_op jit(solution)/shard_map/ppermute | solution.py:49
  94.1 36.5 %collective-permute-start.10 = (bf16[4800,128]{1,0:T(8,128)(2,1)}, bf16[4800,128]{1,0:T(8,128)(2,1)}, u32[]{:S(2)}, u32[]{:S(2)}) collective-permute-start(bf16[4800,128]{1,0:T(8,128)(2,1)} %collective-permute-done.refs_1_), channel_id=1, source_target_pairs={{1,0},{2,1},{3,2},{0,3},{5,4},{6,5},{7,6},{4,7},{9,8},{10,9},{11,1... | collective-permute-start | bytes 3686408 | tf_op jit(solution)/shard_map/ppermute | solution.py:54
  94.4 36.2 %collective-permute-start.11 = (bf16[4800,128]{1,0:T(8,128)(2,1)}, bf16[4800,128]{1,0:T(8,128)(2,1)}, u32[]{:S(2)}, u32[]{:S(2)}) collective-permute-start(bf16[4800,128]{1,0:T(8,128)(2,1)} %collective-permute-done.2.refs_3_), channel_id=1, source_target_pairs={{4,0},{8,4},{12,8},{0,12},{5,1},{9,5},{13,9},{1,13},{6,2},{10,6},{... | collective-permute-start | bytes 3686408 | tf_op jit(solution)/shard_map/ppermute | solution.py:54
  95.2 35.4 %collective-permute-start.12 = (bf16[4800,128]{1,0:T(8,128)(2,1)}, bf16[4800,128]{1,0:T(8,128)(2,1)}, u32[]{:S(2)}, u32[]{:S(2)}) collective-permute-start(bf16[4800,128]{1,0:T(8,128)(2,1)} %collective-permute-done.7.refs_2_), channel_id=1, source_target_pairs={{3,0},{0,1},{1,2},{2,3},{7,4},{4,5},{5,6},{6,7},{11,8},{8,9},{9,10... | collective-permute-start | bytes 3686408 | tf_op jit(solution)/shard_map/ppermute | solution.py:54
  96.1 34.5 %collective-permute-start.13 = (bf16[4800,128]{1,0:T(8,128)(2,1)}, bf16[4800,128]{1,0:T(8,128)(2,1)}, u32[]{:S(2)}, u32[]{:S(2)}) collective-permute-start(bf16[4800,128]{1,0:T(8,128)(2,1)} %collective-permute-done.8.refs_3_), channel_id=1, source_target_pairs={{12,0},{0,4},{4,8},{8,12},{13,1},{1,5},{5,9},{9,13},{14,2},{2,6},{... | collective-permute-start | bytes 3686408 | tf_op jit(solution)/shard_map/ppermute | solution.py:54
  97.9 1.9 copy-start.1
  105.9 1.6 copy-start.2
  111.5 19.1 %all-to-all-start.3 = ((f32[8,2,4800]{2,1,0:T(2,128)}), f32[8,2,4800]{2,1,0:T(2,128)S(1)}, u32[]{:S(2)}, u32[]{:S(2)}) async-start(f32[8,2,4800]{2,1,0:T(2,128)} %reshape.30), calls=%async_computation.3 | async-start | bytes 622592 | tf_op jit(solution)/shard_map/all_to_all | solution.py:207
  131.7 14.5 %all-to-all-start.4 = ((f32[16,2,4800]{2,1,0:T(2,128)}), f32[16,2,4800]{2,1,0:T(2,128)}, u32[]{:S(2)}, u32[]{:S(2)}) async-start(f32[16,2,4800]{2,1,0:T(2,128)} %broadcast_in_dim.20), calls=%async_computation.4 | async-start | bytes 1245184 | tf_op jit(solution)/shard_map/all_to_all | solution.py:45
  136.5 32.2 %collective-permute-start.14 = (bf16[4800,128]{1,0:T(8,128)(2,1)}, bf16[4800,128]{1,0:T(8,128)(2,1)S(1)}, u32[]{:S(2)}, u32[]{:S(2)}) collective-permute-start(bf16[4800,128]{1,0:T(8,128)(2,1)} %collective-permute-done.8.refs_3_), channel_id=1, source_target_pairs={{1,0},{2,1},{3,2},{0,3},{5,4},{6,5},{7,6},{4,7},{9,8},{10,9},{11,1... | collective-permute-start | bytes 3686408 | tf_op jit(solution)/shard_map/ppermute | solution.py:54
  139.0 34.1 %collective-permute-start.15 = (bf16[4800,128]{1,0:T(8,128)(2,1)}, bf16[4800,128]{1,0:T(8,128)(2,1)}, u32[]{:S(2)}, u32[]{:S(2)}) collective-permute-start(bf16[4800,128]{1,0:T(8,128)(2,1)} %collective-permute-done.12.refs_2_), channel_id=1, source_target_pairs={{4,0},{8,4},{12,8},{0,12},{5,1},{9,5},{13,9},{1,13},{6,2},{10,6},{... | collective-permute-start | bytes 3686408 | tf_op jit(solution)/shard_map/ppermute | solution.py:54
  141.4 32.6 %collective-permute-start.16 = (bf16[4800,128]{1,0:T(8,128)(2,1)}, bf16[4800,128]{1,0:T(8,128)(2,1)}, u32[]{:S(2)}, u32[]{:S(2)}) collective-permute-start(bf16[4800,128]{1,0:T(8,128)(2,1)} %collective-permute-done.6.refs_1_), channel_id=1, source_target_pairs={{12,0},{0,4},{4,8},{8,12},{13,1},{1,5},{5,9},{9,13},{14,2},{2,6},{... | collective-permute-start | bytes 3686408 | tf_op jit(solution)/shard_map/ppermute | solution.py:54
  148.4 17.4 %all-to-all-start.5 = ((f32[8,2,4800]{2,1,0:T(2,128)}), f32[8,2,4800]{2,1,0:T(2,128)}, u32[]{:S(2)}, u32[]{:S(2)}) async-start(f32[8,2,4800]{2,1,0:T(2,128)} %broadcast_in_dim.21), calls=%async_computation.5 | async-start | bytes 622592 | tf_op jit(solution)/shard_map/all_to_all | solution.py:45
  156.0 1.9 copy-start.3
  164.1 1.6 copy-start.4
  175.9 3.1 %collective-permute-start.17 = (f32[16,4800]{1,0:T(8,128)}, f32[16,4800]{1,0:T(8,128)S(1)}, u32[]{:S(2)}, u32[]{:S(2)}) collective-permute-start(f32[16,4800]{1,0:T(8,128)} %reshape.31), channel_id=1, source_target_pairs={{0,16},{16,0},{1,17},{17,1},{2,18},{18,2},{3,19},{19,3},{4,20},{20... | collective-permute-start | bytes 921608 | tf_op jit(solution)/shard_map/ppermute | solution.py:49
  180.1 2.1 %copy-start.5 = (f32[160,4800]{1,0:T(8,128)S(1)}, f32[160,4800]{1,0:T(8,128)}, u32[]{:S(2)}) copy-start(f32[160,4800]{1,0:T(8,128)} %copy-done.4) | copy-start | bytes 9216004
  182.2 1.8 copy-start.7

commit v2 on v0

--- a/solution.py
+++ b/solution.py
@@ -55,60 +55,49 @@
 
 
 def products(n, where, pre_ref, weight_ref, *refs):
-    blocks, held, (mat_ref, grad_ref, pre_buf, weight_buf, sems) = refs[:n], refs[n:-5], refs[-5:]
-    fetch_pre = pltpu.make_async_copy(pre_ref, pre_buf, sems.at[0])
-    fetch_weight = pltpu.make_async_copy(weight_ref, weight_buf, sems.at[1])
-    fetch_pre.start()
-    fetch_weight.start()
+    blocks, held, (mat_ref, grad_ref) = refs[:n], refs[n:-2], refs[-2:]
     if held:
         grad_ref[...] = held[1][...]
+    rows = grad_ref.shape[0]
     own = blocks[0].shape[1]
     spots = [pl.ds(pl.multiple_of(where[i] * own, own), own) for i in range(n)]
-    fetch_pre.wait()
-    pre = jnp.concatenate([pre_buf[:, s] for s in spots], axis=1).astype(F32)
+    pre = jnp.concatenate([pre_ref[:, s] for s in spots], axis=1).astype(F32)
     act, pull = jax.vjp(jax.nn.gelu, pre)
     act = act.astype(BF16)
-    fetch_weight.wait()
-    feat = weight_buf.shape[1]
+    feat = weight_ref.shape[1]
     back = jnp.zeros(pre.shape, F32)
     for lo in range(0, feat, 512):
         part = slice(lo, min(feat, lo + 512))
         piece = jnp.concatenate([b[part, :] for b in blocks], axis=1)
-        back = back + dot(weight_buf[:, part], piece, 1, 0)
+        back = back + dot(weight_ref[:, part], piece, 1, 0)
         more = dot(act, piece, 1, 1)
         mat_ref[:, part] = more + held[0][:, part] if held else more
     out = pull(back)[0].astype(BF16)
     for i, s in enumerate(spots):
-        grad_ref[:, s] = out[:, i * own:(i + 1) * own]
-
-
-def add_products(where, pre_act, weight, blocks, held):
+        grad_ref[:, s] = out[:rows, i * own:(i + 1) * own]
+
+
+def add_products(where, rows, pre, weight, blocks, held):
     vmem = pl.BlockSpec(memory_space=pltpu.VMEM)
     n = len(blocks)
     mat = jax.ShapeDtypeStruct(weight.shape, F32)
     return pl.pallas_call(
         functools.partial(products, n),
-        out_shape=(mat, jax.ShapeDtypeStruct(pre_act.shape, BF16)),
-        in_specs=[pl.BlockSpec(memory_space=pltpu.SMEM)]
-        + [pl.BlockSpec(memory_space=pltpu.HBM)] * 2
-        + [vmem] * (n + len(held)),
+        out_shape=(mat, jax.ShapeDtypeStruct((rows, pre.shape[1]), BF16)),
+        in_specs=[pl.BlockSpec(memory_space=pltpu.SMEM)] + [vmem] * (n + 2 + len(held)),
         out_specs=(vmem, vmem),
-        scratch_shapes=[
-            pltpu.VMEM(pre_act.shape, BF16),
-            pltpu.VMEM(weight.shape, BF16),
-            pltpu.SemaphoreType.DMA((2,)),
-        ],
         input_output_aliases={n + 3: 0, n + 4: 1} if held else {},
-        compiler_params=pltpu.CompilerParams(vmem_limit_bytes=12 * 2**20),
-    )(where, pre_act, weight, *blocks, *held)
+        compiler_params=pltpu.CompilerParams(vmem_limit_bytes=9 * 2**20),
+    )(where, pre, weight, *blocks, *held)
 
 
 def finish(mat_ref, error_ref, left_ref, right_ref, out_ref):
-    feat = mat_ref.shape[1]
+    rows, _, feat = error_ref.shape
     left = left_ref[...]
     for lo in range(0, feat, 512):
         part = slice(lo, min(feat, lo + 512))
-        out_ref[:, 0, part] = mat_ref[:, part] + error_ref[:, 0, part] - dot(left, right_ref[:, part], 1, 0)
+        low_rank = dot(left, right_ref[:, part], 1, 0)
+        out_ref[:, 0, part] = mat_ref[:, part][:rows] + error_ref[:, 0, part] - low_rank
 
 
 def new_errors(mat, error, left, right):
@@ -137,7 +126,7 @@
         out_shape=jax.ShapeDtypeStruct(more.shape, F32),
         in_specs=[vmem] * 3,
         out_specs=vmem,
-        compiler_params=pltpu.CompilerParams(vmem_limit_bytes=12 * 2**20),
+        compiler_params=pltpu.CompilerParams(vmem_limit_bytes=8 * 2**20),
     )(z2, og, more)
 
 
@@ -173,9 +162,12 @@
             state[:] = out[2]
         return out[0]
 
+    pad = ((0, -hid % 16), (0, 0))
+    pre_pad, w_pad = jnp.pad(pre_act, pad), jnp.pad(weight, pad)
+
     def use(keys):
         where = jnp.stack([((iy + dy) & (ny - 1)) * nx + ((ix + dx) & (nx - 1)) for dy, dx in keys])
-        state[:] = add_products(where, pre_act, weight, [got[k] for k in keys], state)
+        state[:] = add_products(where, hid, pre_pad, w_pad, [got[k] for k in keys], state)
 
     one = fetch(((0, 0), "x", 1), ((0, 0), "x", -1), ((0, 0), "y", 1), ((0, 0), "y", -1))
 
@@ -233,11 +225,11 @@
     q_t = jnp.dot(inv, r_all, precision=hi)
     phat = jnp.dot(inv, pbar, precision=hi)
 
-    mat, pre_grad = state
     ph, pw = split(phat, 2)
     qh, ql = split(q_t, 2)
     left = jnp.concatenate([ph, ph, pw], axis=0).T
     right = jnp.concatenate([qh, ql, qh], axis=0)
+    mat, pre_grad = state
     new_error = new_errors(mat, error[:, None], left, right).transpose(1, 0, 2)
     return (pre_grad, new_error, q_t.T)
 

time: 185 us -> 186 us (level)
  starting transfers between devices: 67.7 us -> 63.6 us
  waiting for transfers between devices: 37.6 us -> 41 us
  local copies, waits for them, and re-layouts: 20.6 us -> 23.7 us
  Pallas kernels: 31.4 us -> 28.4 us
    pallas_call x4, Pallas kernels: 27.8 us -> 24.7 us  [add_products(): pl.pallas_call(functools.partial(products, n), out_shape=(mat, jax.ShapeD...]
    ppermute x3, starting transfers between devices: 10.1 us -> 7.2 us  [other_core(): return lax.ppermute(x, 'core', [(0, 1), (1, 0)])]
    pad x0 -> x2, local copies, waits for them, and re-layouts: none -> 2.19 us  [shards(): pre_pad, w_pad = (jnp.pad(pre_act, pad), jnp.pad(weight, pad))]
    ppermute x15, waiting for transfers between devices: 10.7 us -> 12.8 us  [shift(): return lax.ppermute(x, axis, [((i + step) % n, i) for i in range(n)])]
  transfers between devices with their start and end apart: 24 -> 24, of which waited for: 10 -> 10; matrix products, arithmetic and copies ran while one was open for 13% -> 15% of each run, Pallas kernels for 15% -> 13%
where the time goes in v2:
time: 186 us; the launch traced here: 185 us
  starting transfers between devices  63.6 us (34%)
  waiting for transfers between devices  41 us (22%)
  Pallas kernels  28.4 us (15%)
  local copies, waits for them, and re-layouts  23.7 us (13%)
  other arithmetic  15 us (8%)
  matrix products  11.9 us (6%)
    all_to_all x4, starting transfers between devices, spread(): lax.all_to_all(jnp.broadcast_to(x, (n,) + x.shape), axis, 0, 0, tiled=True)  26.5 us
    pallas_call x4, Pallas kernels, add_products(): pl.pallas_call(functools.partial(products, n), out_shape=(mat, jax.ShapeD...  24.7 us
    ppermute x15, starting transfers between devices, shift(): return lax.ppermute(x, axis, [((i + step) % n, i) for i in range(n)])  18.6 us
    all_to_all x4, waiting for transfers between devices, spread(): lax.all_to_all(jnp.broadcast_to(x, (n,) + x.shape), axis, 0, 0, tiled=True)  18.6 us
    unnamed x42, local copies, waits for them, and re-layouts  14.6 us
    ppermute x15, waiting for transfers between devices, shift(): return lax.ppermute(x, axis, [((i + step) % n, i) for i in range(n)])  12.8 us
    dot_general x6, matrix products, dot(): lax.dot_general(a, b, (((ca,), (cb,)), ((), ())), preferred_element_type=...  9.28 us
    all_to_all x1, starting transfers between devices, shards(): lax.all_to_all(keep.reshape(nz, half // nz, feat), 'z', 0, 0, tiled=True)  7.56 us
  transfers between devices with their start and end apart: 24, of which 10 were waited for; matrix products, arithmetic and copies ran while one was open for 15% of the time, Pallas kernels for 13%

profile of v2, /device:TPU:1, one launch (start us, length us, event | category | flops | bytes accessed | tf_op | source)
XLA Modules:
  0.0 184.7 jit_solution(11610385074248120817)
XLA Ops:
  0.6 3.4 %collective-permute-start = (bf16[4800,128]{1,0:T(8,128)(2,1)}, bf16[4800,128]{1,0:T(8,128)(2,1)}, u32[]{:S(2)}, u32[]{:S(2)}) collective-permute-start(bf16[4800,128]{1,0:T(8,128)(2,1)} %bitcast.58), channel_id=1, source_target_pairs={{1,0},{2,1},{3,2},{0,3},{5,4},{6,5},{7,6},{4,7},{9,8},{10,9},{11,1... | collective-permute-start | bytes 3686408 | tf_op jit(solution)/shard_map/ppermute | solution.py:54
  4.0 2.7 %collective-permute-start.2 = (bf16[4800,128]{1,0:T(8,128)(2,1)}, bf16[4800,128]{1,0:T(8,128)(2,1)}, u32[]{:S(2)}, u32[]{:S(2)}) collective-permute-start(bf16[4800,128]{1,0:T(8,128)(2,1)} %bitcast.60), channel_id=1, source_target_pairs={{4,0},{8,4},{12,8},{0,12},{5,1},{9,5},{13,9},{1,13},{6,2},{10,6},{... | collective-permute-start | bytes 3686408 | tf_op jit(solution)/shard_map/ppermute | solution.py:54
  6.8 1.3 reduce-precision_convert_fusion.2
  8.1 1.7 fusion.27
  10.5 6.5 %all-to-all-start = ((f32[16,32,128]{2,1,0:T(8,128)}), f32[16,32,128]{2,1,0:T(8,128)}, u32[]{:S(2)}, u32[]{:S(2)}) async-start(f32[16,32,128]{2,1,0:T(8,128)} %broadcast_in_dim.17), calls=%async_computation | async-start | bytes 524288 | tf_op jit(solution)/shard_map/all_to_all | solution.py:45
  17.0 1.3 fusion.19
  18.2 1.3 fusion.2
  19.5 18.0 %all-to-all-done = f32[16,32,128]{2,1,0:T(8,128)} async-done(((f32[16,32,128]{2,1,0:T(8,128)}), f32[16,32,128]{2,1,0:T(8,128)}, u32[]{:S(2)}, u32[]{:S(2)}) %all-to-all-start) | async-done | bytes 262176 | tf_op jit(solution)/shard_map/all_to_all | solution.py:45
  39.1 3.0 %collective-permute-start.8 = (bf16[4800,128]{1,0:T(8,128)(2,1)}, bf16[4800,128]{1,0:T(8,128)(2,1)}, u32[]{:S(2)}, u32[]{:S(2)}) collective-permute-start(bf16[4800,128]{1,0:T(8,128)(2,1)} %collective-permute-done.3.refs_4_), channel_id=1, source_target_pairs={{1,0},{2,1},{3,2},{0,3},{5,4},{6,5},{7,6},{4,7},{9,8},{10,9},{11,1... | collective-permute-start | bytes 3686408 | tf_op jit(solution)/shard_map/ppermute | solution.py:54
  43.2 1.7 fusion.23
  45.7 8.2 %all-to-all-start.1 = ((f32[8,32,150]{2,1,0:T(8,128)}), f32[8,32,150]{2,1,0:T(8,128)S(1)}, u32[]{:S(2)}, u32[]{:S(2)}) async-start(f32[8,32,150]{2,1,0:T(8,128)} %broadcast_in_dim.18), calls=%async_computation.1 | async-start | bytes 524288 | tf_op jit(solution)/shard_map/all_to_all | solution.py:45
  54.8 1.2 pad.9.weight_ref
  56.2 1.4 copy-done
  57.6 1.1 copy-done.7
  58.7 1.3 copy-done.11
  59.9 6.7 %shard_map.76 = (f32[160,4800]{1,0:T(8,128)S(1)}, bf16[150,2048]{1,0:T(8,128)(2,1)}) custom-call(s32[5]{0:T(128)S(1)} %stack.69.where, bf16[160,2048]{1,0:T(8,128)(2,1)S(1)} %copy-done.7, bf16[160,4800]{1,0:T(8,128)(2,1)S(1)} %copy-done, bf16[4800,128]{1,0:T(8,128)(2,1)S(1)} %bitcast.62, bf16[4800,128]{1,0:T(8,128)(2,1)} %collective-permute-done.refs_1_, ...), custom_call_target="tpu_custom_call" | custom-call | tf_op jit(solution)/shard_map/pallas_call | solution.py:84
  66.6 4.3 %collective-permute-start.4 = (f32[32,150]{1,0:T(8,128)S(1)}, f32[32,150]{1,0:T(8,128)S(1)}, u32[]{:S(2)}, u32[]{:S(2)}) collective-permute-start(f32[32,150]{1,0:T(8,128)S(1)} %reduce_sum.36), channel_id=1, source_target_pairs={{0,16},{16,0},{1,17},{17,1},{2,18},{18,2},{3,19},{19,3},{4,20},{20... | collective-permute-start | bytes 57608 | tf_op jit(solution)/shard_map/ppermute | solution.py:49
  72.0 1.8 fusion.32
  74.0 1.5 fusion.18
  76.5 3.8 %all-to-all-start.2 = ((f32[16,40,128]{2,1,0:T(8,128)}), f32[16,40,128]{2,1,0:T(8,128)S(1)}, u32[]{:S(2)}, u32[]{:S(2)}) async-start(f32[16,40,128]{2,1,0:T(8,128)} %pad_maximum_fusion.2), calls=%async_computation.2 | async-start | bytes 655360 | tf_op jit(solution)/shard_map/all_to_all | solution.py:201
  80.3 2.2 %slice_add_fusion.more_ref = f32[32,4800]{1,0:T(8,128)} fusion(f32[64,4800]{1,0:T(8,128)} %fusion.18), kind=kLoop, calls=%fused_computation.24 | loop fusion | flops 153600 | bytes 1843200 | tf_op jit(solution)/shard_map/add | solution.py:40
  82.4 6.6 %all-to-all-done.2 = f32[16,40,128]{2,1,0:T(8,128)S(1)} async-done(((f32[16,40,128]{2,1,0:T(8,128)}), f32[16,40,128]{2,1,0:T(8,128)S(1)}, u32[]{:S(2)}, u32[]{:S(2)}) %all-to-all-start.2) | async-done | bytes 327712 | tf_op jit(solution)/shard_map/all_to_all | solution.py:201
  89.1 1.3 copy-done.12
  92.1 1.6 collective-permute-start.9
  97.6 7.6 %all-to-all-start.3 = ((f32[8,2,4800]{2,1,0:T(2,128)}), f32[8,2,4800]{2,1,0:T(2,128)S(1)}, u32[]{:S(2)}, u32[]{:S(2)}) async-start(f32[8,2,4800]{2,1,0:T(2,128)} %reshape.30), calls=%async_computation.3 | async-start | bytes 622592 | tf_op jit(solution)/shard_map/all_to_all | solution.py:212
  105.3 1.4 copy-done.1
  106.7 1.1 copy-done.8
  107.7 6.2 %shard_map.78 = (f32[160,4800]{1,0:T(8,128)S(1)}, bf16[150,2048]{1,0:T(8,128)(2,1)}) custom-call(s32[4]{0:T(128)S(1)} %pad_add_fusion.1.where, bf16[160,2048]{1,0:T(8,128)(2,1)S(1)} %copy-done.8, bf16[160,4800]{1,0:T(8,128)(2,1)S(1)} %copy-done.1, bf16[4800,128]{1,0:T(8,128)(2,1)} %collective-permute-done.5.refs_0_, ...), custom_call_target="tpu_custom_call", output_to_operand_aliasing={{0}: (7, {}), {1}: (8, {})} | custom-call | tf_op jit(solution)/shard_map/pallas_call | solution.py:84
  114.0 2.1 %all-to-all-done.3 = f32[8,2,4800]{2,1,0:T(2,128)S(1)} async-done(((f32[8,2,4800]{2,1,0:T(2,128)}), f32[8,2,4800]{2,1,0:T(2,128)S(1)}, u32[]{:S(2)}, u32[]{:S(2)}) %all-to-all-start.3) | async-done | bytes 307232 | tf_op jit(solution)/shard_map/all_to_all | solution.py:212
  116.1 6.5 %collective-permute-done.10.refs_0_ = bf16[4800,128]{1,0:T(8,128)(2,1)} collective-permute-done((bf16[4800,128]{1,0:T(8,128)(2,1)}, bf16[4800,128]{1,0:T(8,128)(2,1)}, u32[]{:S(2)}, u32[]{:S(2)}) %collective-permute-start.10) | collective-permute-done | bytes 1228832 | tf_op jit(solution)/shard_map/ppermute | solution.py:54
  122.6 1.7 collective-permute-done.12.refs_2_
  126.0 4.3 %all-to-all-start.4 = ((f32[16,2,4800]{2,1,0:T(2,128)}), f32[16,2,4800]{2,1,0:T(2,128)}, u32[]{:S(2)}, u32[]{:S(2)}) async-start(f32[16,2,4800]{2,1,0:T(2,128)} %broadcast_in_dim.20), calls=%async_computation.4 | async-start | bytes 1245184 | tf_op jit(solution)/shard_map/all_to_all | solution.py:45
  130.9 2.4 %collective-permute-start.14 = (bf16[4800,128]{1,0:T(8,128)(2,1)}, bf16[4800,128]{1,0:T(8,128)(2,1)}, u32[]{:S(2)}, u32[]{:S(2)}) collective-permute-start(bf16[4800,128]{1,0:T(8,128)(2,1)} %collective-permute-done.8.refs_3_), channel_id=1, source_target_pairs={{1,0},{2,1},{3,2},{0,3},{5,4},{6,5},{7,6},{4,7},{9,8},{10,9},{11,1... | collective-permute-start | bytes 3686408 | tf_op jit(solution)/shard_map/ppermute | solution.py:54
  133.3 2.5 %collective-permute-start.15 = (bf16[4800,128]{1,0:T(8,128)(2,1)}, bf16[4800,128]{1,0:T(8,128)(2,1)}, u32[]{:S(2)}, u32[]{:S(2)}) collective-permute-start(bf16[4800,128]{1,0:T(8,128)(2,1)} %collective-permute-done.12.refs_2_), channel_id=1, source_target_pairs={{4,0},{8,4},{12,8},{0,12},{5,1},{9,5},{13,9},{1,13},{6,2},{10,6},{... | collective-permute-start | bytes 3686408 | tf_op jit(solution)/shard_map/ppermute | solution.py:54
  135.8 1.4 copy-done.2
  137.2 1.1 copy-done.9
  138.3 6.2 %shard_map.79 = (f32[160,4800]{1,0:T(8,128)S(1)}, bf16[150,2048]{1,0:T(8,128)(2,1)}) custom-call(s32[4]{0:T(128)S(1)} %pad_add_fusion.2.where, bf16[160,2048]{1,0:T(8,128)(2,1)S(1)} %copy-done.9, bf16[160,4800]{1,0:T(8,128)(2,1)S(1)} %copy-done.2, bf16[4800,128]{1,0:T(8,128)(2,1)} %collective-permute-done.10.refs_0_, ...), custom_call_target="tpu_custom_call", output_to_operand_aliasing={{0}: (7, {}), {1}: (8, {})} | custom-call | tf_op jit(solution)/shard_map/pallas_call | solution.py:84
  144.5 1.3 reduce_sum.39
  146.6 7.6 %all-to-all-start.5 = ((f32[8,2,4800]{2,1,0:T(2,128)}), f32[8,2,4800]{2,1,0:T(2,128)S(1)}, u32[]{:S(2)}, u32[]{:S(2)}) async-start(f32[8,2,4800]{2,1,0:T(2,128)} %broadcast_in_dim.21), calls=%async_computation.5 | async-start | bytes 622592 | tf_op jit(solution)/shard_map/all_to_all | solution.py:45
  154.2 2.9 %cholesky.17 = f32[32,32]{1,0:T(8,128)S(1)} custom-call(f32[32,32]{1,0:T(8,128)S(1)} %fusion.38), custom_call_target="Cholesky" | custom-call | tf_op jit(solution)/shard_map/jit(cholesky)/cholesky | solution.py:218
  158.5 2.4 %custom-call.7 = f32[1,32,32]{1,2,0:T(8,128)S(1)} custom-call(f32[1,32,32]{2,1,0:T(8,128)S(1)} %fusion.33), custom_call_target="InvertDiagBlocksLowerTriangular" | custom-call | tf_op jit(solution)/shard_map/jit(_solve_triangular)/triangular_solve | solution.py:219
  164.2 2.7 %collective-permute-done.15.refs_1_ = bf16[4800,128]{1,0:T(8,128)(2,1)} collective-permute-done((bf16[4800,128]{1,0:T(8,128)(2,1)}, bf16[4800,128]{1,0:T(8,128)(2,1)}, u32[]{:S(2)}, u32[]{:S(2)}) %collective-permute-start.15) | collective-permute-done | bytes 1228832 | tf_op jit(solution)/shard_map/ppermute | solution.py:54
  166.9 1.2 collective-permute-done.16.refs_2_
  169.0 1.3 collective-permute-start.17
  171.3 1.4 copy-done.3
  173.8 5.7 %shard_map.80 = (f32[160,4800]{1,0:T(8,128)S(1)}, bf16[150,2048]{1,0:T(8,128)(2,1)}) custom-call(s32[3]{0:T(128)S(1)} %pad_add_fusion.where, bf16[160,2048]{1,0:T(8,128)(2,1)S(1)} %copy-done.10, bf16[160,4800]{1,0:T(8,128)(2,1)S(1)} %copy-done.3, bf16[4800,128]{1,0:T(8,128)(2,1)} %collective-permute-done.14.refs_0_, ...), custom_call_target="tpu_custom_call", output_to_operand_aliasing={{0}: (6, {}), {1}: (7, {})} | custom-call | tf_op jit(solution)/shard_map/pallas_call | solution.py:84
  179.5 1.5 fusion.13
  181.6 3.1 %shard_map.81 = f32[150,1,4800]{2,1,0:T(1,128)} custom-call(f32[160,4800]{1,0:T(8,128)S(1)} %get-tuple-element.90.mat_ref, f32[150,1,4800]{2,1,0:T(1,128)S(1)} %bitcast.57, bf16[150,96]{1,0:T(8,128)(2,1)S(1)} %maximum_bitcast_fusion.left_ref, bf16[96,4800]{1,0:T(8,128)(2,1)S(1)} %pad_maximum_fusion.right_ref), custom_call_target="tpu_custom_call" | custom-call | tf_op jit(solution)/shard_map/pallas_call | solution.py:105
  (106 shorter events, 24.3 us)
Async XLA Ops:
  0.6 36.9 %collective-permute-start = (bf16[4800,128]{1,0:T(8,128)(2,1)}, bf16[4800,128]{1,0:T(8,128)(2,1)}, u32[]{:S(2)}, u32[]{:S(2)}) collective-permute-start(bf16[4800,128]{1,0:T(8,128)(2,1)} %bitcast.58), channel_id=1, source_target_pairs={{1,0},{2,1},{3,2},{0,3},{5,4},{6,5},{7,6},{4,7},{9,8},{10,9},{11,1... | collective-permute-start | bytes 3686408 | tf_op jit(solution)/shard_map/ppermute | solution.py:54
  4.0 33.5 %collective-permute-start.1 = (bf16[4800,128]{1,0:T(8,128)(2,1)}, bf16[4800,128]{1,0:T(8,128)(2,1)}, u32[]{:S(2)}, u32[]{:S(2)}) collective-permute-start(bf16[4800,128]{1,0:T(8,128)(2,1)} %bitcast.59), channel_id=1, source_target_pairs={{3,0},{0,1},{1,2},{2,3},{7,4},{4,5},{5,6},{6,7},{11,8},{8,9},{9,10... | collective-permute-start | bytes 3686408 | tf_op jit(solution)/shard_map/ppermute | solution.py:54
  4.0 33.5 %collective-permute-start.2 = (bf16[4800,128]{1,0:T(8,128)(2,1)}, bf16[4800,128]{1,0:T(8,128)(2,1)}, u32[]{:S(2)}, u32[]{:S(2)}) collective-permute-start(bf16[4800,128]{1,0:T(8,128)(2,1)} %bitcast.60), channel_id=1, source_target_pairs={{4,0},{8,4},{12,8},{0,12},{5,1},{9,5},{13,9},{1,13},{6,2},{10,6},{... | collective-permute-start | bytes 3686408 | tf_op jit(solution)/shard_map/ppermute | solution.py:54
  6.8 30.7 %collective-permute-start.3 = (bf16[4800,128]{1,0:T(8,128)(2,1)}, bf16[4800,128]{1,0:T(8,128)(2,1)}, u32[]{:S(2)}, u32[]{:S(2)}) collective-permute-start(bf16[4800,128]{1,0:T(8,128)(2,1)} %bitcast.61), channel_id=1, source_target_pairs={{12,0},{0,4},{4,8},{8,12},{13,1},{1,5},{5,9},{9,13},{14,2},{2,6},{... | collective-permute-start | bytes 3686408 | tf_op jit(solution)/shard_map/ppermute | solution.py:54
  6.8 10.2 %copy-start.4 = (f32[1,150,4800]{2,0,1:T(1,128)S(1)}, f32[1,150,4800]{2,0,1:T(1,128)}, u32[]{:S(2)}) copy-start(f32[1,150,4800]{2,0,1:T(1,128)} %param.8) | copy-start | bytes 8640004
  10.5 27.0 %all-to-all-start = ((f32[16,32,128]{2,1,0:T(8,128)}), f32[16,32,128]{2,1,0:T(8,128)}, u32[]{:S(2)}, u32[]{:S(2)}) async-start(f32[16,32,128]{2,1,0:T(8,128)} %broadcast_in_dim.17), calls=%async_computation | async-start | bytes 524288 | tf_op jit(solution)/shard_map/all_to_all | solution.py:45
  37.5 34.3 %collective-permute-start.5 = (bf16[4800,128]{1,0:T(8,128)(2,1)}, bf16[4800,128]{1,0:T(8,128)(2,1)}, u32[]{:S(2)}, u32[]{:S(2)}) collective-permute-start(bf16[4800,128]{1,0:T(8,128)(2,1)} %collective-permute-done.refs_1_), channel_id=1, source_target_pairs={{4,0},{8,4},{12,8},{0,12},{5,1},{9,5},{13,9},{1,13},{6,2},{10,6},{... | collective-permute-start | bytes 3686408 | tf_op jit(solution)/shard_map/ppermute | solution.py:54
  38.6 33.2 %collective-permute-start.7 = (bf16[4800,128]{1,0:T(8,128)(2,1)}, bf16[4800,128]{1,0:T(8,128)(2,1)}, u32[]{:S(2)}, u32[]{:S(2)}) collective-permute-start(bf16[4800,128]{1,0:T(8,128)(2,1)} %collective-permute-done.2.refs_3_), channel_id=1, source_target_pairs={{3,0},{0,1},{1,2},{2,3},{7,4},{4,5},{5,6},{6,7},{11,8},{8,9},{9,10... | collective-permute-start | bytes 3686408 | tf_op jit(solution)/shard_map/ppermute | solution.py:54
  38.6 33.2 %collective-permute-start.6 = (bf16[4800,128]{1,0:T(8,128)(2,1)}, bf16[4800,128]{1,0:T(8,128)(2,1)}, u32[]{:S(2)}, u32[]{:S(2)}) collective-permute-start(bf16[4800,128]{1,0:T(8,128)(2,1)} %collective-permute-done.1.refs_2_), channel_id=1, source_target_pairs={{12,0},{0,4},{4,8},{8,12},{13,1},{1,5},{5,9},{9,13},{14,2},{2,6},{... | collective-permute-start | bytes 3686408 | tf_op jit(solution)/shard_map/ppermute | solution.py:54
  39.1 32.7 %collective-permute-start.8 = (bf16[4800,128]{1,0:T(8,128)(2,1)}, bf16[4800,128]{1,0:T(8,128)(2,1)}, u32[]{:S(2)}, u32[]{:S(2)}) collective-permute-start(bf16[4800,128]{1,0:T(8,128)(2,1)} %collective-permute-done.3.refs_4_), channel_id=1, source_target_pairs={{1,0},{2,1},{3,2},{0,3},{5,4},{6,5},{7,6},{4,7},{9,8},{10,9},{11,1... | collective-permute-start | bytes 3686408 | tf_op jit(solution)/shard_map/ppermute | solution.py:54
  43.1 1.8 copy-start.17
  43.1 1.8 copy-start.18
  43.2 10.7 %copy-start.16 = (bf16[150,2048]{1,0:T(8,128)(2,1)S(1)}, bf16[150,2048]{1,0:T(8,128)(2,1)}, u32[]{:S(2)}) copy-start(bf16[150,2048]{1,0:T(8,128)(2,1)} %param.5) | copy-start | bytes 1843204
  44.9 9.9 %copy-start.14 = (bf16[150,4800]{1,0:T(8,128)(2,1)S(1)}, bf16[150,4800]{1,0:T(8,128)(2,1)}, u32[]{:S(2)}) copy-start(bf16[150,4800]{1,0:T(8,128)(2,1)} %param.7) | copy-start | bytes 4320004
  45.7 20.9 %all-to-all-start.1 = ((f32[8,32,150]{2,1,0:T(8,128)}), f32[8,32,150]{2,1,0:T(8,128)S(1)}, u32[]{:S(2)}, u32[]{:S(2)}) async-start(f32[8,32,150]{2,1,0:T(8,128)} %broadcast_in_dim.18), calls=%async_computation.1 | async-start | bytes 524288 | tf_op jit(solution)/shard_map/all_to_all | solution.py:45
  56.2 1.4 copy-start
  57.6 1.1 copy-start.7
  58.6 1.3 copy-start.11
  66.6 5.1 %collective-permute-start.4 = (f32[32,150]{1,0:T(8,128)S(1)}, f32[32,150]{1,0:T(8,128)S(1)}, u32[]{:S(2)}, u32[]{:S(2)}) collective-permute-start(f32[32,150]{1,0:T(8,128)S(1)} %reduce_sum.36), channel_id=1, source_target_pairs={{0,16},{16,0},{1,17},{17,1},{2,18},{18,2},{3,19},{19,3},{4,20},{20... | collective-permute-start | bytes 57608 | tf_op jit(solution)/shard_map/ppermute | solution.py:49
  72.0 2.0 %copy-start.5 = (f32[1,150,4800]{2,0,1:T(1,128)S(1)}, f32[1,150,4800]{2,0,1:T(1,128)}, u32[]{:S(2)}) copy-start(f32[1,150,4800]{2,0,1:T(1,128)} %param.8) | copy-start | bytes 8640004
  76.5 12.6 %all-to-all-start.2 = ((f32[16,40,128]{2,1,0:T(8,128)}), f32[16,40,128]{2,1,0:T(8,128)S(1)}, u32[]{:S(2)}, u32[]{:S(2)}) async-start(f32[16,40,128]{2,1,0:T(8,128)} %pad_maximum_fusion.2), calls=%async_computation.2 | async-start | bytes 655360 | tf_op jit(solution)/shard_map/all_to_all | solution.py:201
  89.1 1.3 copy-start.12
  90.4 1.1 copy-start.13
  92.1 4.6 %collective-permute-start.9 = (f32[16,4800]{1,0:T(8,128)S(1)}, f32[16,4800]{1,0:T(8,128)S(1)}, u32[]{:S(2)}, u32[]{:S(2)}) collective-permute-start(f32[16,4800]{1,0:T(8,128)S(1)} %slice_select_fusion), channel_id=1, source_target_pairs={{0,16},{16,0},{1,17},{17,1},{2,18},{18,2},{3,19},{19,3},{4,20},{20... | collective-permute-start | bytes 921608 | tf_op jit(solution)/shard_map/ppermute | solution.py:49
  93.7 28.9 %collective-permute-start.10 = (bf16[4800,128]{1,0:T(8,128)(2,1)}, bf16[4800,128]{1,0:T(8,128)(2,1)}, u32[]{:S(2)}, u32[]{:S(2)}) collective-permute-start(bf16[4800,128]{1,0:T(8,128)(2,1)} %collective-permute-done.refs_1_), channel_id=1, source_target_pairs={{1,0},{2,1},{3,2},{0,3},{5,4},{6,5},{7,6},{4,7},{9,8},{10,9},{11,1... | collective-permute-start | bytes 3686408 | tf_op jit(solution)/shard_map/ppermute | solution.py:54
  94.0 28.6 %collective-permute-start.11 = (bf16[4800,128]{1,0:T(8,128)(2,1)}, bf16[4800,128]{1,0:T(8,128)(2,1)}, u32[]{:S(2)}, u32[]{:S(2)}) collective-permute-start(bf16[4800,128]{1,0:T(8,128)(2,1)} %collective-permute-done.2.refs_3_), channel_id=1, source_target_pairs={{4,0},{8,4},{12,8},{0,12},{5,1},{9,5},{13,9},{1,13},{6,2},{10,6},{... | collective-permute-start | bytes 3686408 | tf_op jit(solution)/shard_map/ppermute | solution.py:54
  94.9 29.5 %collective-permute-start.12 = (bf16[4800,128]{1,0:T(8,128)(2,1)}, bf16[4800,128]{1,0:T(8,128)(2,1)}, u32[]{:S(2)}, u32[]{:S(2)}) collective-permute-start(bf16[4800,128]{1,0:T(8,128)(2,1)} %collective-permute-done.7.refs_2_), channel_id=1, source_target_pairs={{3,0},{0,1},{1,2},{2,3},{7,4},{4,5},{5,6},{6,7},{11,8},{8,9},{9,10... | collective-permute-start | bytes 3686408 | tf_op jit(solution)/shard_map/ppermute | solution.py:54
  95.8 29.1 %collective-permute-start.13 = (bf16[4800,128]{1,0:T(8,128)(2,1)}, bf16[4800,128]{1,0:T(8,128)(2,1)}, u32[]{:S(2)}, u32[]{:S(2)}) collective-permute-start(bf16[4800,128]{1,0:T(8,128)(2,1)} %collective-permute-done.8.refs_3_), channel_id=1, source_target_pairs={{12,0},{0,4},{4,8},{8,12},{13,1},{1,5},{5,9},{9,13},{14,2},{2,6},{... | collective-permute-start | bytes 3686408 | tf_op jit(solution)/shard_map/ppermute | solution.py:54
  97.6 18.5 %all-to-all-start.3 = ((f32[8,2,4800]{2,1,0:T(2,128)}), f32[8,2,4800]{2,1,0:T(2,128)S(1)}, u32[]{:S(2)}, u32[]{:S(2)}) async-start(f32[8,2,4800]{2,1,0:T(2,128)} %reshape.30), calls=%async_computation.3 | async-start | bytes 622592 | tf_op jit(solution)/shard_map/all_to_all | solution.py:212
  105.3 1.4 copy-start.1
  106.7 1.1 copy-start.8
  126.0 18.5 %all-to-all-start.4 = ((f32[16,2,4800]{2,1,0:T(2,128)}), f32[16,2,4800]{2,1,0:T(2,128)}, u32[]{:S(2)}, u32[]{:S(2)}) async-start(f32[16,2,4800]{2,1,0:T(2,128)} %broadcast_in_dim.20), calls=%async_computation.4 | async-start | bytes 1245184 | tf_op jit(solution)/shard_map/all_to_all | solution.py:45
  130.9 33.2 %collective-permute-start.14 = (bf16[4800,128]{1,0:T(8,128)(2,1)}, bf16[4800,128]{1,0:T(8,128)(2,1)}, u32[]{:S(2)}, u32[]{:S(2)}) collective-permute-start(bf16[4800,128]{1,0:T(8,128)(2,1)} %collective-permute-done.8.refs_3_), channel_id=1, source_target_pairs={{1,0},{2,1},{3,2},{0,3},{5,4},{6,5},{7,6},{4,7},{9,8},{10,9},{11,1... | collective-permute-start | bytes 3686408 | tf_op jit(solution)/shard_map/ppermute | solution.py:54
  133.3 33.6 %collective-permute-start.15 = (bf16[4800,128]{1,0:T(8,128)(2,1)}, bf16[4800,128]{1,0:T(8,128)(2,1)}, u32[]{:S(2)}, u32[]{:S(2)}) collective-permute-start(bf16[4800,128]{1,0:T(8,128)(2,1)} %collective-permute-done.12.refs_2_), channel_id=1, source_target_pairs={{4,0},{8,4},{12,8},{0,12},{5,1},{9,5},{13,9},{1,13},{6,2},{10,6},{... | collective-permute-start | bytes 3686408 | tf_op jit(solution)/shard_map/ppermute | solution.py:54
  135.8 32.3 %collective-permute-start.16 = (bf16[4800,128]{1,0:T(8,128)(2,1)}, bf16[4800,128]{1,0:T(8,128)(2,1)}, u32[]{:S(2)}, u32[]{:S(2)}) collective-permute-start(bf16[4800,128]{1,0:T(8,128)(2,1)} %collective-permute-done.6.refs_1_), channel_id=1, source_target_pairs={{12,0},{0,4},{4,8},{8,12},{13,1},{1,5},{5,9},{9,13},{14,2},{2,6},{... | collective-permute-start | bytes 3686408 | tf_op jit(solution)/shard_map/ppermute | solution.py:54
  135.8 1.4 copy-start.2
  137.2 1.1 copy-start.9
  146.6 17.5 %all-to-all-start.5 = ((f32[8,2,4800]{2,1,0:T(2,128)}), f32[8,2,4800]{2,1,0:T(2,128)S(1)}, u32[]{:S(2)}, u32[]{:S(2)}) async-start(f32[8,2,4800]{2,1,0:T(2,128)} %broadcast_in_dim.21), calls=%async_computation.5 | async-start | bytes 622592 | tf_op jit(solution)/shard_map/all_to_all | solution.py:45
  169.0 10.4 %collective-permute-start.17 = (f32[16,4800]{1,0:T(8,128)}, f32[16,4800]{1,0:T(8,128)S(1)}, u32[]{:S(2)}, u32[]{:S(2)}) collective-permute-start(f32[16,4800]{1,0:T(8,128)} %reshape.31), channel_id=1, source_target_pairs={{0,16},{16,0},{1,17},{17,1},{2,18},{18,2},{3,19},{19,3},{4,20},{20... | collective-permute-start | bytes 921608 | tf_op jit(solution)/shard_map/ppermute | solution.py:49
  171.3 1.4 copy-start.3
  172.7 1.1 copy-start.10
  173.8 5.7 %copy-start.15 = (f32[16,4800]{1,0:T(8,128)S(1)}, f32[16,4800]{1,0:T(8,128)}, u32[]{:S(2)}) copy-start(f32[16,4800]{1,0:T(8,128)} %reshape.31) | copy-start | bytes 921604
  179.5 2.1 %copy-start.6 = (f32[1,150,4800]{2,0,1:T(1,128)S(1)}, f32[1,150,4800]{2,0,1:T(1,128)}, u32[]{:S(2)}) copy-start(f32[1,150,4800]{2,0,1:T(1,128)} %param.8) | copy-start | bytes 8640004

commit v3 on v2

--- a/solution.py
+++ b/solution.py
@@ -87,7 +87,7 @@
         in_specs=[pl.BlockSpec(memory_space=pltpu.SMEM)] + [vmem] * (n + 2 + len(held)),
         out_specs=(vmem, vmem),
         input_output_aliases={n + 3: 0, n + 4: 1} if held else {},
-        compiler_params=pltpu.CompilerParams(vmem_limit_bytes=9 * 2**20),
+        compiler_params=pltpu.CompilerParams(vmem_limit_bytes=12 * 2**20),
     )(where, pre, weight, *blocks, *held)
 
 
@@ -126,7 +126,7 @@
         out_shape=jax.ShapeDtypeStruct(more.shape, F32),
         in_specs=[vmem] * 3,
         out_specs=vmem,
-        compiler_params=pltpu.CompilerParams(vmem_limit_bytes=8 * 2**20),
+        compiler_params=pltpu.CompilerParams(vmem_limit_bytes=12 * 2**20),
     )(z2, og, more)
 
 
@@ -162,12 +162,9 @@
             state[:] = out[2]
         return out[0]
 
-    pad = ((0, -hid % 16), (0, 0))
-    pre_pad, w_pad = jnp.pad(pre_act, pad), jnp.pad(weight, pad)
-
     def use(keys):
         where = jnp.stack([((iy + dy) & (ny - 1)) * nx + ((ix + dx) & (nx - 1)) for dy, dx in keys])
-        state[:] = add_products(where, hid, pre_pad, w_pad, [got[k] for k in keys], state)
+        state[:] = add_products(where, hid, pre_act, weight, [got[k] for k in keys], state)
 
     one = fetch(((0, 0), "x", 1), ((0, 0), "x", -1), ((0, 0), "y", 1), ((0, 0), "y", -1))
 

time: 186 us -> 184 us (0.989)
  starting transfers between devices: 63.6 us -> 68.3 us
  local copies, waits for them, and re-layouts: 23.7 us -> 20.6 us
  waiting for transfers between devices: 41 us -> 39 us
    ppermute x3, starting transfers between devices: 7.2 us -> 10.6 us  [other_core(): return lax.ppermute(x, 'core', [(0, 1), (1, 0)])]
    pad x2 -> x0, local copies, waits for them, and re-layouts: 2.19 us -> none  [shards(): pre_pad, w_pad = (jnp.pad(pre_act, pad), jnp.pad(weight, pad))]
  transfers between devices with their start and end apart: 24 -> 24, of which waited for: 10 -> 10; matrix products, arithmetic and copies ran while one was open for 15% -> 13% of each run, Pallas kernels for 13% -> 14%
where the time goes in v3:
time: 184 us; the launch traced here: 183 us
  starting transfers between devices  68.3 us (37%)
  waiting for transfers between devices  39 us (21%)
  Pallas kernels  28.6 us (16%)
  local copies, waits for them, and re-layouts  20.6 us (11%)
  other arithmetic  13.2 us (7%)
  matrix products  12.3 us (7%)
    all_to_all x4, starting transfers between devices, spread(): lax.all_to_all(jnp.broadcast_to(x, (n,) + x.shape), axis, 0, 0, tiled=True)  27.1 us
    pallas_call x4, Pallas kernels, add_products(): pl.pallas_call(functools.partial(products, n), out_shape=(mat, jax.ShapeD...  24.9 us
    all_to_all x4, waiting for transfers between devices, spread(): lax.all_to_all(jnp.broadcast_to(x, (n,) + x.shape), axis, 0, 0, tiled=True)  18.9 us
    ppermute x15, starting transfers between devices, shift(): return lax.ppermute(x, axis, [((i + step) % n, i) for i in range(n)])  18.6 us
    unnamed x42, local copies, waits for them, and re-layouts  15.1 us
    ppermute x15, waiting for transfers between devices, shift(): return lax.ppermute(x, axis, [((i + step) % n, i) for i in range(n)])  11.4 us
    ppermute x3, starting transfers between devices, other_core(): return lax.ppermute(x, 'core', [(0, 1), (1, 0)])  10.6 us
    dot_general x6, matrix products, dot(): lax.dot_general(a, b, (((ca,), (cb,)), ((), ())), preferred_element_type=...  10.2 us
  transfers between devices with their start and end apart: 24, of which 10 were waited for; matrix products, arithmetic and copies ran while one was open for 13% of the time, Pallas kernels for 14%

profile of v3, /device:TPU:1, one launch (start us, length us, event | category | flops | bytes accessed | tf_op | source)
XLA Modules:
  0.0 182.9 jit_solution(15540439523224733739)
XLA Ops:
  0.6 3.4 %collective-permute-start = (bf16[4800,128]{1,0:T(8,128)(2,1)}, bf16[4800,128]{1,0:T(8,128)(2,1)}, u32[]{:S(2)}, u32[]{:S(2)}) collective-permute-start(bf16[4800,128]{1,0:T(8,128)(2,1)} %bitcast.58), channel_id=1, source_target_pairs={{1,0},{2,1},{3,2},{0,3},{5,4},{6,5},{7,6},{4,7},{9,8},{10,9},{11,1... | collective-permute-start | bytes 3686408 | tf_op jit(solution)/shard_map/ppermute | solution.py:54
  4.0 2.7 %collective-permute-start.2 = (bf16[4800,128]{1,0:T(8,128)(2,1)}, bf16[4800,128]{1,0:T(8,128)(2,1)}, u32[]{:S(2)}, u32[]{:S(2)}) collective-permute-start(bf16[4800,128]{1,0:T(8,128)(2,1)} %bitcast.60), channel_id=1, source_target_pairs={{4,0},{8,4},{12,8},{0,12},{5,1},{9,5},{13,9},{1,13},{6,2},{10,6},{... | collective-permute-start | bytes 3686408 | tf_op jit(solution)/shard_map/ppermute | solution.py:54
  6.8 1.3 reduce-precision_convert_fusion.2
  8.8 1.7 fusion.27
  11.2 6.4 %all-to-all-start = ((f32[16,32,128]{2,1,0:T(8,128)}), f32[16,32,128]{2,1,0:T(8,128)S(1)}, u32[]{:S(2)}, u32[]{:S(2)}) async-start(f32[16,32,128]{2,1,0:T(8,128)} %broadcast_in_dim.17), calls=%async_computation | async-start | bytes 524288 | tf_op jit(solution)/shard_map/all_to_all | solution.py:45
  17.7 2.3 %fusion.19 = f32[64,150]{1,0:T(8,128)} fusion(f32[1,150,4800]{2,0,1:T(1,128)S(1)} %copy-done, bf16[4800,32]{0,1:T(8,128)(2,1)} %copy-done.15, bf16[4800,32]{0,1:T(8,128)(2,1)S(1)} %get-tuple-element.97), kind=kOutput, calls=%fused_computation.31 | convolution fusion | flops 94828800 | bytes 3532800 | tf_op jit(solution)/shard_map/dot_general | solution.py:35
  20.0 1.3 fusion.2
  21.2 16.3 %all-to-all-done = f32[16,32,128]{2,1,0:T(8,128)S(1)} async-done(((f32[16,32,128]{2,1,0:T(8,128)}), f32[16,32,128]{2,1,0:T(8,128)S(1)}, u32[]{:S(2)}, u32[]{:S(2)}) %all-to-all-start) | async-done | bytes 262176 | tf_op jit(solution)/shard_map/all_to_all | solution.py:45
  39.1 3.0 %collective-permute-start.8 = (bf16[4800,128]{1,0:T(8,128)(2,1)}, bf16[4800,128]{1,0:T(8,128)(2,1)}, u32[]{:S(2)}, u32[]{:S(2)}) collective-permute-start(bf16[4800,128]{1,0:T(8,128)(2,1)} %collective-permute-done.3.refs_4_), channel_id=1, source_target_pairs={{1,0},{2,1},{3,2},{0,3},{5,4},{6,5},{7,6},{4,7},{9,8},{10,9},{11,1... | collective-permute-start | bytes 3686408 | tf_op jit(solution)/shard_map/ppermute | solution.py:54
  42.2 1.7 fusion.23
  44.7 8.2 %all-to-all-start.1 = ((f32[8,32,150]{2,1,0:T(8,128)}), f32[8,32,150]{2,1,0:T(8,128)S(1)}, u32[]{:S(2)}, u32[]{:S(2)}) async-start(f32[8,32,150]{2,1,0:T(8,128)} %broadcast_in_dim.18), calls=%async_computation.1 | async-start | bytes 524288 | tf_op jit(solution)/shard_map/all_to_all | solution.py:45
  52.9 1.4 copy-done.3
  54.3 1.1 copy-done.7
  55.4 1.3 copy-done.11
  56.7 6.8 %shard_map.76 = (f32[150,4800]{1,0:T(8,128)S(1)}, bf16[150,2048]{1,0:T(8,128)(2,1)}) custom-call(s32[5]{0:T(128)S(1)} %stack.69.where, bf16[150,2048]{1,0:T(8,128)(2,1)S(1)} %copy-done.7, bf16[150,4800]{1,0:T(8,128)(2,1)S(1)} %copy-done.3, bf16[4800,128]{1,0:T(8,128)(2,1)S(1)} %bitcast.62, bf16[4800,128]{1,0:T(8,128)(2,1)} %collective-permute-done.refs_1_, ...), custom_call_target="tpu_custom_call" | custom-call | tf_op jit(solution)/shard_map/pallas_call | solution.py:84
  63.5 4.2 %collective-permute-start.4 = (f32[32,150]{1,0:T(8,128)S(1)}, f32[32,150]{1,0:T(8,128)S(1)}, u32[]{:S(2)}, u32[]{:S(2)}) collective-permute-start(f32[32,150]{1,0:T(8,128)S(1)} %reduce_sum.36), channel_id=1, source_target_pairs={{0,16},{16,0},{1,17},{17,1},{2,18},{18,2},{3,19},{19,3},{4,20},{20... | collective-permute-start | bytes 57608 | tf_op jit(solution)/shard_map/ppermute | solution.py:49
  68.7 1.8 %fusion.32 = f32[64,2048]{1,0:T(8,128)S(1)} fusion(bf16[32,150]{1,0:T(8,128)(2,1)S(1)} %get-tuple-element.104, bf16[32,150]{1,0:T(8,128)(2,1)S(1)} %get-tuple-element.103, bf16[150,2048]{1,0:T(8,128)(2,1)} %pre_ref.7), kind=kOutput, calls=%fused_computation.64 | convolution fusion | flops 42432000 | bytes 1157888 | tf_op jit(solution)/shard_map/dot_general | solution.py:35
  70.7 1.5 fusion.18
  73.2 3.8 %all-to-all-start.2 = ((f32[16,40,128]{2,1,0:T(8,128)}), f32[16,40,128]{2,1,0:T(8,128)S(1)}, u32[]{:S(2)}, u32[]{:S(2)}) async-start(f32[16,40,128]{2,1,0:T(8,128)} %pad_maximum_fusion.2), calls=%async_computation.2 | async-start | bytes 655360 | tf_op jit(solution)/shard_map/all_to_all | solution.py:198
  77.0 2.2 %slice_add_fusion.more_ref = f32[32,4800]{1,0:T(8,128)} fusion(f32[64,4800]{1,0:T(8,128)} %fusion.18), kind=kLoop, calls=%fused_computation.24 | loop fusion | flops 153600 | bytes 1843200 | tf_op jit(solution)/shard_map/add | solution.py:40
  79.1 5.7 %all-to-all-done.2 = f32[16,40,128]{2,1,0:T(8,128)S(1)} async-done(((f32[16,40,128]{2,1,0:T(8,128)}), f32[16,40,128]{2,1,0:T(8,128)S(1)}, u32[]{:S(2)}, u32[]{:S(2)}) %all-to-all-start.2) | async-done | bytes 327712 | tf_op jit(solution)/shard_map/all_to_all | solution.py:198
  84.9 1.3 copy-done.12
  87.9 5.2 %collective-permute-start.9 = (f32[16,4800]{1,0:T(8,128)S(1)}, f32[16,4800]{1,0:T(8,128)S(1)}, u32[]{:S(2)}, u32[]{:S(2)}) collective-permute-start(f32[16,4800]{1,0:T(8,128)S(1)} %slice_select_fusion), channel_id=1, source_target_pairs={{0,16},{16,0},{1,17},{17,1},{2,18},{18,2},{3,19},{19,3},{4,20},{20... | collective-permute-start | bytes 921608 | tf_op jit(solution)/shard_map/ppermute | solution.py:49
  97.0 8.2 %all-to-all-start.3 = ((f32[8,2,4800]{2,1,0:T(2,128)}), f32[8,2,4800]{2,1,0:T(2,128)S(1)}, u32[]{:S(2)}, u32[]{:S(2)}) async-start(f32[8,2,4800]{2,1,0:T(2,128)} %reshape.30), calls=%async_computation.3 | async-start | bytes 622592 | tf_op jit(solution)/shard_map/all_to_all | solution.py:209
  105.2 1.4 copy-done.4
  107.7 6.3 %shard_map.78 = (f32[150,4800]{1,0:T(8,128)S(1)}, bf16[150,2048]{1,0:T(8,128)(2,1)}) custom-call(s32[4]{0:T(128)S(1)} %pad_add_fusion.1.where, bf16[150,2048]{1,0:T(8,128)(2,1)S(1)} %copy-done.8, bf16[150,4800]{1,0:T(8,128)(2,1)S(1)} %copy-done.4, bf16[4800,128]{1,0:T(8,128)(2,1)} %collective-permute-done.5.refs_0_, ...), custom_call_target="tpu_custom_call", output_to_operand_aliasing={{0}: (7, {}), {1}: (8, {})} | custom-call | tf_op jit(solution)/shard_map/pallas_call | solution.py:84
  114.0 2.1 %all-to-all-done.3 = f32[8,2,4800]{2,1,0:T(2,128)S(1)} async-done(((f32[8,2,4800]{2,1,0:T(2,128)}), f32[8,2,4800]{2,1,0:T(2,128)S(1)}, u32[]{:S(2)}, u32[]{:S(2)}) %all-to-all-start.3) | async-done | bytes 307232 | tf_op jit(solution)/shard_map/all_to_all | solution.py:209
  116.1 5.9 %collective-permute-done.10.refs_0_ = bf16[4800,128]{1,0:T(8,128)(2,1)} collective-permute-done((bf16[4800,128]{1,0:T(8,128)(2,1)}, bf16[4800,128]{1,0:T(8,128)(2,1)}, u32[]{:S(2)}, u32[]{:S(2)}) %collective-permute-start.10) | collective-permute-done | bytes 1228832 | tf_op jit(solution)/shard_map/ppermute | solution.py:54
  122.0 1.8 collective-permute-done.12.refs_2_
  125.4 4.3 %all-to-all-start.4 = ((f32[16,2,4800]{2,1,0:T(2,128)}), f32[16,2,4800]{2,1,0:T(2,128)}, u32[]{:S(2)}, u32[]{:S(2)}) async-start(f32[16,2,4800]{2,1,0:T(2,128)} %broadcast_in_dim.20), calls=%async_computation.4 | async-start | bytes 1245184 | tf_op jit(solution)/shard_map/all_to_all | solution.py:45
  130.3 2.4 %collective-permute-start.14 = (bf16[4800,128]{1,0:T(8,128)(2,1)}, bf16[4800,128]{1,0:T(8,128)(2,1)}, u32[]{:S(2)}, u32[]{:S(2)}) collective-permute-start(bf16[4800,128]{1,0:T(8,128)(2,1)} %collective-permute-done.8.refs_3_), channel_id=1, source_target_pairs={{1,0},{2,1},{3,2},{0,3},{5,4},{6,5},{7,6},{4,7},{9,8},{10,9},{11,1... | collective-permute-start | bytes 3686408 | tf_op jit(solution)/shard_map/ppermute | solution.py:54
  132.7 2.5 %collective-permute-start.15 = (bf16[4800,128]{1,0:T(8,128)(2,1)}, bf16[4800,128]{1,0:T(8,128)(2,1)}, u32[]{:S(2)}, u32[]{:S(2)}) collective-permute-start(bf16[4800,128]{1,0:T(8,128)(2,1)} %collective-permute-done.12.refs_2_), channel_id=1, source_target_pairs={{4,0},{8,4},{12,8},{0,12},{5,1},{9,5},{13,9},{1,13},{6,2},{10,6},{... | collective-permute-start | bytes 3686408 | tf_op jit(solution)/shard_map/ppermute | solution.py:54
  135.2 1.4 copy-done.5
  136.5 1.1 copy-done.9
  137.6 6.3 %shard_map.79 = (f32[150,4800]{1,0:T(8,128)S(1)}, bf16[150,2048]{1,0:T(8,128)(2,1)}) custom-call(s32[4]{0:T(128)S(1)} %pad_add_fusion.2.where, bf16[150,2048]{1,0:T(8,128)(2,1)S(1)} %copy-done.9, bf16[150,4800]{1,0:T(8,128)(2,1)S(1)} %copy-done.5, bf16[4800,128]{1,0:T(8,128)(2,1)} %collective-permute-done.10.refs_0_, ...), custom_call_target="tpu_custom_call", output_to_operand_aliasing={{0}: (7, {}), {1}: (8, {})} | custom-call | tf_op jit(solution)/shard_map/pallas_call | solution.py:84
  143.9 1.3 reduce_sum.39
  146.0 8.2 %all-to-all-start.5 = ((f32[8,2,4800]{2,1,0:T(2,128)}), f32[8,2,4800]{2,1,0:T(2,128)S(1)}, u32[]{:S(2)}, u32[]{:S(2)}) async-start(f32[8,2,4800]{2,1,0:T(2,128)} %broadcast_in_dim.21), calls=%async_computation.5 | async-start | bytes 622592 | tf_op jit(solution)/shard_map/all_to_all | solution.py:45
  154.3 2.9 %cholesky.17 = f32[32,32]{1,0:T(8,128)S(1)} custom-call(f32[32,32]{1,0:T(8,128)S(1)} %fusion.38), custom_call_target="Cholesky" | custom-call | tf_op jit(solution)/shard_map/jit(cholesky)/cholesky | solution.py:215
  158.5 2.4 %custom-call.7 = f32[1,32,32]{1,2,0:T(8,128)S(1)} custom-call(f32[1,32,32]{2,1,0:T(8,128)S(1)} %fusion.33), custom_call_target="InvertDiagBlocksLowerTriangular" | custom-call | tf_op jit(solution)/shard_map/jit(_solve_triangular)/triangular_solve | solution.py:216
  161.6 2.6 %all-to-all-done.5 = f32[8,2,4800]{2,1,0:T(2,128)S(1)} async-done(((f32[8,2,4800]{2,1,0:T(2,128)}), f32[8,2,4800]{2,1,0:T(2,128)S(1)}, u32[]{:S(2)}, u32[]{:S(2)}) %all-to-all-start.5) | async-done | bytes 307232 | tf_op jit(solution)/shard_map/all_to_all | solution.py:45
  164.2 2.0 %collective-permute-done.15.refs_1_ = bf16[4800,128]{1,0:T(8,128)(2,1)} collective-permute-done((bf16[4800,128]{1,0:T(8,128)(2,1)}, bf16[4800,128]{1,0:T(8,128)(2,1)}, u32[]{:S(2)}, u32[]{:S(2)}) %collective-permute-start.15) | collective-permute-done | bytes 1228832 | tf_op jit(solution)/shard_map/ppermute | solution.py:54
  166.2 1.2 collective-permute-done.16.refs_2_
  168.3 1.3 collective-permute-start.17
  169.8 1.4 copy-done.6
  171.1 1.1 copy-done.10
  172.2 5.6 %shard_map.80 = (f32[150,4800]{1,0:T(8,128)S(1)}, bf16[150,2048]{1,0:T(8,128)(2,1)}) custom-call(s32[3]{0:T(128)S(1)} %pad_add_fusion.where, bf16[150,2048]{1,0:T(8,128)(2,1)S(1)} %copy-done.10, bf16[150,4800]{1,0:T(8,128)(2,1)S(1)} %copy-done.6, bf16[4800,128]{1,0:T(8,128)(2,1)} %collective-permute-done.14.refs_0_, ...), custom_call_target="tpu_custom_call", output_to_operand_aliasing={{0}: (6, {}), {1}: (7, {})} | custom-call | tf_op jit(solution)/shard_map/pallas_call | solution.py:84
  177.8 1.5 fusion.13
  179.9 3.1 %shard_map.81 = f32[150,1,4800]{2,1,0:T(1,128)} custom-call(f32[150,4800]{1,0:T(8,128)S(1)} %get-tuple-element.90.mat_ref, f32[150,1,4800]{2,1,0:T(1,128)S(1)} %bitcast.57, bf16[150,96]{1,0:T(8,128)(2,1)S(1)} %maximum_bitcast_fusion.left_ref, bf16[96,4800]{1,0:T(8,128)(2,1)S(1)} %pad_maximum_fusion.right_ref), custom_call_target="tpu_custom_call" | custom-call | tf_op jit(solution)/shard_map/pallas_call | solution.py:105
  (104 shorter events, 19.6 us)
Async XLA Ops:
  0.6 36.9 %collective-permute-start = (bf16[4800,128]{1,0:T(8,128)(2,1)}, bf16[4800,128]{1,0:T(8,128)(2,1)}, u32[]{:S(2)}, u32[]{:S(2)}) collective-permute-start(bf16[4800,128]{1,0:T(8,128)(2,1)} %bitcast.58), channel_id=1, source_target_pairs={{1,0},{2,1},{3,2},{0,3},{5,4},{6,5},{7,6},{4,7},{9,8},{10,9},{11,1... | collective-permute-start | bytes 3686408 | tf_op jit(solution)/shard_map/ppermute | solution.py:54
  4.0 33.5 %collective-permute-start.1 = (bf16[4800,128]{1,0:T(8,128)(2,1)}, bf16[4800,128]{1,0:T(8,128)(2,1)}, u32[]{:S(2)}, u32[]{:S(2)}) collective-permute-start(bf16[4800,128]{1,0:T(8,128)(2,1)} %bitcast.59), channel_id=1, source_target_pairs={{3,0},{0,1},{1,2},{2,3},{7,4},{4,5},{5,6},{6,7},{11,8},{8,9},{9,10... | collective-permute-start | bytes 3686408 | tf_op jit(solution)/shard_map/ppermute | solution.py:54
  4.0 33.5 %collective-permute-start.2 = (bf16[4800,128]{1,0:T(8,128)(2,1)}, bf16[4800,128]{1,0:T(8,128)(2,1)}, u32[]{:S(2)}, u32[]{:S(2)}) collective-permute-start(bf16[4800,128]{1,0:T(8,128)(2,1)} %bitcast.60), channel_id=1, source_target_pairs={{4,0},{8,4},{12,8},{0,12},{5,1},{9,5},{13,9},{1,13},{6,2},{10,6},{... | collective-permute-start | bytes 3686408 | tf_op jit(solution)/shard_map/ppermute | solution.py:54
  6.8 30.7 %collective-permute-start.3 = (bf16[4800,128]{1,0:T(8,128)(2,1)}, bf16[4800,128]{1,0:T(8,128)(2,1)}, u32[]{:S(2)}, u32[]{:S(2)}) collective-permute-start(bf16[4800,128]{1,0:T(8,128)(2,1)} %bitcast.61), channel_id=1, source_target_pairs={{12,0},{0,4},{4,8},{8,12},{13,1},{1,5},{5,9},{9,13},{14,2},{2,6},{... | collective-permute-start | bytes 3686408 | tf_op jit(solution)/shard_map/ppermute | solution.py:54
  6.8 10.9 %copy-start = (f32[1,150,4800]{2,0,1:T(1,128)S(1)}, f32[1,150,4800]{2,0,1:T(1,128)}, u32[]{:S(2)}) copy-start(f32[1,150,4800]{2,0,1:T(1,128)} %param.8) | copy-start | bytes 8640004
  8.1 0.7 copy-start.15
  11.2 26.3 %all-to-all-start = ((f32[16,32,128]{2,1,0:T(8,128)}), f32[16,32,128]{2,1,0:T(8,128)S(1)}, u32[]{:S(2)}, u32[]{:S(2)}) async-start(f32[16,32,128]{2,1,0:T(8,128)} %broadcast_in_dim.17), calls=%async_computation | async-start | bytes 524288 | tf_op jit(solution)/shard_map/all_to_all | solution.py:45
  17.7 2.3 %copy-start.16 = (bf16[4800,32]{0,1:T(8,128)(2,1)S(1)}, bf16[4800,32]{0,1:T(8,128)(2,1)}, u32[]{:S(2)}) copy-start(bf16[4800,32]{0,1:T(8,128)(2,1)} %copy-done.15) | copy-start | bytes 921604
  37.5 31.0 %collective-permute-start.5 = (bf16[4800,128]{1,0:T(8,128)(2,1)}, bf16[4800,128]{1,0:T(8,128)(2,1)}, u32[]{:S(2)}, u32[]{:S(2)}) collective-permute-start(bf16[4800,128]{1,0:T(8,128)(2,1)} %collective-permute-done.refs_1_), channel_id=1, source_target_pairs={{4,0},{8,4},{12,8},{0,12},{5,1},{9,5},{13,9},{1,13},{6,2},{10,6},{... | collective-permute-start | bytes 3686408 | tf_op jit(solution)/shard_map/ppermute | solution.py:54
  38.6 29.9 %collective-permute-start.7 = (bf16[4800,128]{1,0:T(8,128)(2,1)}, bf16[4800,128]{1,0:T(8,128)(2,1)}, u32[]{:S(2)}, u32[]{:S(2)}) collective-permute-start(bf16[4800,128]{1,0:T(8,128)(2,1)} %collective-permute-done.2.refs_3_), channel_id=1, source_target_pairs={{3,0},{0,1},{1,2},{2,3},{7,4},{4,5},{5,6},{6,7},{11,8},{8,9},{9,10... | collective-permute-start | bytes 3686408 | tf_op jit(solution)/shard_map/ppermute | solution.py:54
  38.6 29.9 %collective-permute-start.6 = (bf16[4800,128]{1,0:T(8,128)(2,1)}, bf16[4800,128]{1,0:T(8,128)(2,1)}, u32[]{:S(2)}, u32[]{:S(2)}) collective-permute-start(bf16[4800,128]{1,0:T(8,128)(2,1)} %collective-permute-done.1.refs_2_), channel_id=1, source_target_pairs={{12,0},{0,4},{4,8},{8,12},{13,1},{1,5},{5,9},{9,13},{14,2},{2,6},{... | collective-permute-start | bytes 3686408 | tf_op jit(solution)/shard_map/ppermute | solution.py:54
  39.1 29.4 %collective-permute-start.8 = (bf16[4800,128]{1,0:T(8,128)(2,1)}, bf16[4800,128]{1,0:T(8,128)(2,1)}, u32[]{:S(2)}, u32[]{:S(2)}) collective-permute-start(bf16[4800,128]{1,0:T(8,128)(2,1)} %collective-permute-done.3.refs_4_), channel_id=1, source_target_pairs={{1,0},{2,1},{3,2},{0,3},{5,4},{6,5},{7,6},{4,7},{9,8},{10,9},{11,1... | collective-permute-start | bytes 3686408 | tf_op jit(solution)/shard_map/ppermute | solution.py:54
  42.2 1.7 copy-start.17
  42.2 1.7 copy-start.18
  44.7 18.8 %all-to-all-start.1 = ((f32[8,32,150]{2,1,0:T(8,128)}), f32[8,32,150]{2,1,0:T(8,128)S(1)}, u32[]{:S(2)}, u32[]{:S(2)}) async-start(f32[8,32,150]{2,1,0:T(8,128)} %broadcast_in_dim.18), calls=%async_computation.1 | async-start | bytes 524288 | tf_op jit(solution)/shard_map/all_to_all | solution.py:45
  52.9 1.4 copy-start.3
  54.3 1.1 copy-start.7
  55.4 1.3 copy-start.11
  63.5 5.0 %collective-permute-start.4 = (f32[32,150]{1,0:T(8,128)S(1)}, f32[32,150]{1,0:T(8,128)S(1)}, u32[]{:S(2)}, u32[]{:S(2)}) collective-permute-start(f32[32,150]{1,0:T(8,128)S(1)} %reduce_sum.36), channel_id=1, source_target_pairs={{0,16},{16,0},{1,17},{17,1},{2,18},{18,2},{3,19},{19,3},{4,20},{20... | collective-permute-start | bytes 57608 | tf_op jit(solution)/shard_map/ppermute | solution.py:49
  68.7 2.0 %copy-start.1 = (f32[1,150,4800]{2,0,1:T(1,128)S(1)}, f32[1,150,4800]{2,0,1:T(1,128)}, u32[]{:S(2)}) copy-start(f32[1,150,4800]{2,0,1:T(1,128)} %param.8) | copy-start | bytes 8640004
  73.2 11.7 %all-to-all-start.2 = ((f32[16,40,128]{2,1,0:T(8,128)}), f32[16,40,128]{2,1,0:T(8,128)S(1)}, u32[]{:S(2)}, u32[]{:S(2)}) async-start(f32[16,40,128]{2,1,0:T(8,128)} %pad_maximum_fusion.2), calls=%async_computation.2 | async-start | bytes 655360 | tf_op jit(solution)/shard_map/all_to_all | solution.py:198
  84.9 1.3 copy-start.12
  86.2 1.1 copy-start.13
  87.9 8.1 %collective-permute-start.9 = (f32[16,4800]{1,0:T(8,128)S(1)}, f32[16,4800]{1,0:T(8,128)S(1)}, u32[]{:S(2)}, u32[]{:S(2)}) collective-permute-start(f32[16,4800]{1,0:T(8,128)S(1)} %slice_select_fusion), channel_id=1, source_target_pairs={{0,16},{16,0},{1,17},{17,1},{2,18},{18,2},{3,19},{19,3},{4,20},{20... | collective-permute-start | bytes 921608 | tf_op jit(solution)/shard_map/ppermute | solution.py:49
  93.1 28.9 %collective-permute-start.10 = (bf16[4800,128]{1,0:T(8,128)(2,1)}, bf16[4800,128]{1,0:T(8,128)(2,1)}, u32[]{:S(2)}, u32[]{:S(2)}) collective-permute-start(bf16[4800,128]{1,0:T(8,128)(2,1)} %collective-permute-done.refs_1_), channel_id=1, source_target_pairs={{1,0},{2,1},{3,2},{0,3},{5,4},{6,5},{7,6},{4,7},{9,8},{10,9},{11,1... | collective-permute-start | bytes 3686408 | tf_op jit(solution)/shard_map/ppermute | solution.py:54
  93.4 28.6 %collective-permute-start.11 = (bf16[4800,128]{1,0:T(8,128)(2,1)}, bf16[4800,128]{1,0:T(8,128)(2,1)}, u32[]{:S(2)}, u32[]{:S(2)}) collective-permute-start(bf16[4800,128]{1,0:T(8,128)(2,1)} %collective-permute-done.2.refs_3_), channel_id=1, source_target_pairs={{4,0},{8,4},{12,8},{0,12},{5,1},{9,5},{13,9},{1,13},{6,2},{10,6},{... | collective-permute-start | bytes 3686408 | tf_op jit(solution)/shard_map/ppermute | solution.py:54
  94.3 29.5 %collective-permute-start.12 = (bf16[4800,128]{1,0:T(8,128)(2,1)}, bf16[4800,128]{1,0:T(8,128)(2,1)}, u32[]{:S(2)}, u32[]{:S(2)}) collective-permute-start(bf16[4800,128]{1,0:T(8,128)(2,1)} %collective-permute-done.7.refs_2_), channel_id=1, source_target_pairs={{3,0},{0,1},{1,2},{2,3},{7,4},{4,5},{5,6},{6,7},{11,8},{8,9},{9,10... | collective-permute-start | bytes 3686408 | tf_op jit(solution)/shard_map/ppermute | solution.py:54
  95.1 29.1 %collective-permute-start.13 = (bf16[4800,128]{1,0:T(8,128)(2,1)}, bf16[4800,128]{1,0:T(8,128)(2,1)}, u32[]{:S(2)}, u32[]{:S(2)}) collective-permute-start(bf16[4800,128]{1,0:T(8,128)(2,1)} %collective-permute-done.8.refs_3_), channel_id=1, source_target_pairs={{12,0},{0,4},{4,8},{8,12},{13,1},{1,5},{5,9},{9,13},{14,2},{2,6},{... | collective-permute-start | bytes 3686408 | tf_op jit(solution)/shard_map/ppermute | solution.py:54
  97.0 19.1 %all-to-all-start.3 = ((f32[8,2,4800]{2,1,0:T(2,128)}), f32[8,2,4800]{2,1,0:T(2,128)S(1)}, u32[]{:S(2)}, u32[]{:S(2)}) async-start(f32[8,2,4800]{2,1,0:T(2,128)} %reshape.30), calls=%async_computation.3 | async-start | bytes 622592 | tf_op jit(solution)/shard_map/all_to_all | solution.py:209
  105.2 1.4 copy-start.4
  106.6 1.1 copy-start.8
  125.4 18.6 %all-to-all-start.4 = ((f32[16,2,4800]{2,1,0:T(2,128)}), f32[16,2,4800]{2,1,0:T(2,128)}, u32[]{:S(2)}, u32[]{:S(2)}) async-start(f32[16,2,4800]{2,1,0:T(2,128)} %broadcast_in_dim.20), calls=%async_computation.4 | async-start | bytes 1245184 | tf_op jit(solution)/shard_map/all_to_all | solution.py:45
  130.3 33.9 %collective-permute-start.14 = (bf16[4800,128]{1,0:T(8,128)(2,1)}, bf16[4800,128]{1,0:T(8,128)(2,1)}, u32[]{:S(2)}, u32[]{:S(2)}) collective-permute-start(bf16[4800,128]{1,0:T(8,128)(2,1)} %collective-permute-done.8.refs_3_), channel_id=1, source_target_pairs={{1,0},{2,1},{3,2},{0,3},{5,4},{6,5},{7,6},{4,7},{9,8},{10,9},{11,1... | collective-permute-start | bytes 3686408 | tf_op jit(solution)/shard_map/ppermute | solution.py:54
  132.7 33.6 %collective-permute-start.15 = (bf16[4800,128]{1,0:T(8,128)(2,1)}, bf16[4800,128]{1,0:T(8,128)(2,1)}, u32[]{:S(2)}, u32[]{:S(2)}) collective-permute-start(bf16[4800,128]{1,0:T(8,128)(2,1)} %collective-permute-done.12.refs_2_), channel_id=1, source_target_pairs={{4,0},{8,4},{12,8},{0,12},{5,1},{9,5},{13,9},{1,13},{6,2},{10,6},{... | collective-permute-start | bytes 3686408 | tf_op jit(solution)/shard_map/ppermute | solution.py:54
  135.1 32.3 %collective-permute-start.16 = (bf16[4800,128]{1,0:T(8,128)(2,1)}, bf16[4800,128]{1,0:T(8,128)(2,1)}, u32[]{:S(2)}, u32[]{:S(2)}) collective-permute-start(bf16[4800,128]{1,0:T(8,128)(2,1)} %collective-permute-done.6.refs_1_), channel_id=1, source_target_pairs={{12,0},{0,4},{4,8},{8,12},{13,1},{1,5},{5,9},{9,13},{14,2},{2,6},{... | collective-permute-start | bytes 3686408 | tf_op jit(solution)/shard_map/ppermute | solution.py:54
  135.2 1.4 copy-start.5
  136.5 1.1 copy-start.9
  146.0 18.2 %all-to-all-start.5 = ((f32[8,2,4800]{2,1,0:T(2,128)}), f32[8,2,4800]{2,1,0:T(2,128)S(1)}, u32[]{:S(2)}, u32[]{:S(2)}) async-start(f32[8,2,4800]{2,1,0:T(2,128)} %broadcast_in_dim.21), calls=%async_computation.5 | async-start | bytes 622592 | tf_op jit(solution)/shard_map/all_to_all | solution.py:45
  168.3 9.4 %collective-permute-start.17 = (f32[16,4800]{1,0:T(8,128)}, f32[16,4800]{1,0:T(8,128)S(1)}, u32[]{:S(2)}, u32[]{:S(2)}) collective-permute-start(f32[16,4800]{1,0:T(8,128)} %reshape.31), channel_id=1, source_target_pairs={{0,16},{16,0},{1,17},{17,1},{2,18},{18,2},{3,19},{19,3},{4,20},{20... | collective-permute-start | bytes 921608 | tf_op jit(solution)/shard_map/ppermute | solution.py:49
  169.8 1.4 copy-start.6
  171.1 1.1 copy-start.10
  172.2 5.6 %copy-start.14 = (f32[16,4800]{1,0:T(8,128)S(1)}, f32[16,4800]{1,0:T(8,128)}, u32[]{:S(2)}) copy-start(f32[16,4800]{1,0:T(8,128)} %reshape.31) | copy-start | bytes 921604
  177.8 2.1 %copy-start.2 = (f32[1,150,4800]{2,0,1:T(1,128)S(1)}, f32[1,150,4800]{2,0,1:T(1,128)}, u32[]{:S(2)}) copy-start(f32[1,150,4800]{2,0,1:T(1,128)} %param.8) | copy-start | bytes 8640004
